TPU v7x, 256 devices: a whole 4x4x8 slice. The times are simulated.
256 devices in a mesh: dp: 8 (over y, core), expert: 32 (over z, x).
Axes of the slice: x: 4, y: 4, z: 8, core: 2. Of those that a mesh axis runs over, the one named last changes fastest.
Arguments:
- tokens: bfloat16 [32768, 2048], P(('dp', 'expert')), may hold values from -6 to 6
- cotangent: bfloat16 [32768, 2048], P(('dp', 'expert')), may hold values from -4 to 4
- expert_ids: int32 [32768, 6], P(('dp', 'expert')), may hold values from 0 to 31, all different within a row; in each aligned block of 128 rows (0 to 127, 128 to 255, ...) at most 26 rows name the same one
- gate_values: float32 [32768, 6], P(('dp', 'expert')), may hold values from 0.05 to 0.45
- saved_pre: bfloat16 [32, 8, 32, 26, 1408], P('expert', 'dp'), may hold values from -6 to 6
- w_gate: bfloat16 [32, 2048, 704], P('expert', 'dp'), may hold values from -0.125 to 0.125
- w_up: bfloat16 [32, 2048, 704], P('expert', 'dp'), may hold values from -0.125 to 0.125
- w_down: bfloat16 [32, 704, 2048], P('expert', None, 'dp'), may hold values from -0.21875 to 0.21875
Outputs:
- grad_tokens: bfloat16 [32768, 2048], P(('dp', 'expert'))
- grad_gate: bfloat16 [32, 2048, 704], P('expert', 'dp')
- grad_up: bfloat16 [32, 2048, 704], P('expert', 'dp')
- grad_down: bfloat16 [32, 704, 2048], P('expert', None, 'dp')
Inputs may be any that keep to these rules, and one draw needn't show every extreme that they name: `expert_ids`: each row names 6 different experts; the rows of one device name no expert more than 26 times, a bound that some block reaches.
All inputs are finite; a program needn't handle non-finite values.
Results may differ from a plain program's by a relative error of at most 0.019.
Values may be sent and summed in bfloat16 or wider, within the bound.
A program may use at most 128 MiB of HBM per device.

v0:
```python
import jax
import jax.numpy as jnp
from jax import lax
from jax.sharding import PartitionSpec as P


def shards(tokens, cotangent, expert_ids, gate_values, saved_pre, w_gate, w_up, w_down):
    tok_count, top_k = expert_ids.shape
    experts = lax.axis_size("expert")
    capacity = saved_pre.shape[3]
    feat_width = tokens.shape[1]
    hidden = w_gate.shape[2]
    flat_ids = expert_ids.reshape(-1)
    onehot = (flat_ids[:, None] == jnp.arange(experts, dtype=jnp.int32)[None, :]).astype(jnp.int32)
    before = jnp.cumsum(onehot, axis=0) - onehot
    slot_index = jnp.sum(before * onehot, axis=1)
    target = flat_ids * capacity + slot_index
    source_row = jnp.arange(tok_count * top_k, dtype=jnp.int32) // top_k
    slot_token = jnp.zeros((experts * capacity,), jnp.int32).at[target].set(source_row)
    filled = jnp.zeros((experts * capacity,), jnp.bool_).at[target].set(True)
    slot_gate = (
        jnp.zeros((experts * capacity,), jnp.float32).at[target].set(gate_values.reshape(-1))
    )
    send_rows = jnp.where(filled[:, None], tokens[slot_token], jnp.zeros((), tokens.dtype))
    send_grads = (slot_gate[:, None] * cotangent[slot_token].astype(jnp.float32)).astype(
        jnp.bfloat16
    )
    send_rows = send_rows.reshape(experts, capacity, feat_width)
    send_grads = send_grads.reshape(experts, capacity, feat_width)
    arrived_rows, arrived_grads = (
        lax.all_to_all(send_rows, "expert", split_axis=0, concat_axis=0, tiled=True),
        lax.all_to_all(send_grads, "expert", split_axis=0, concat_axis=0, tiled=True),
    )
    slot_rows = arrived_rows.reshape(-1, feat_width)
    slot_grads = arrived_grads.reshape(-1, feat_width)
    gate_full, up_full = (
        lax.all_gather(w_gate, "dp", axis=1, tiled=True),
        lax.all_gather(w_up, "dp", axis=1, tiled=True),
    )
    gate_full = gate_full[0]
    up_full = up_full[0]
    pre_act = saved_pre.reshape(-1, 2 * hidden).astype(jnp.float32)
    pre_gate = pre_act[:, :hidden]
    pre_up = pre_act[:, hidden:]
    sigmoid_gate = 1.0 / (1.0 + jnp.exp(-pre_gate))
    hidden_act = (pre_gate * sigmoid_gate * pre_up).astype(jnp.bfloat16)
    row_contract = (((1,), (1,)), ((), ()))
    down_full = lax.all_gather(w_down, "dp", axis=2, tiled=True)[0]
    grad_hidden = lax.dot_general(
        slot_grads, down_full, row_contract, preferred_element_type=jnp.float32
    )
    grad_gate_pre = (
        grad_hidden * pre_up * sigmoid_gate * (1.0 + pre_gate * (1.0 - sigmoid_gate))
    ).astype(jnp.bfloat16)
    grad_up_pre = (grad_hidden * pre_gate * sigmoid_gate).astype(jnp.bfloat16)
    slot_back = lax.dot_general(
        grad_gate_pre, gate_full, row_contract, preferred_element_type=jnp.float32
    ) + lax.dot_general(grad_up_pre, up_full, row_contract, preferred_element_type=jnp.float32)
    slot_back = slot_back.astype(jnp.bfloat16).reshape(experts, capacity, feat_width)
    slot_contract = (((0,), (0,)), ((), ()))
    returned = lax.all_to_all(slot_back, "expert", split_axis=0, concat_axis=0, tiled=True)
    flat_back = returned.reshape(-1, feat_width)
    picked = flat_back[target].reshape(tok_count, top_k, feat_width).astype(jnp.float32)
    grad_tokens = jnp.sum(picked, axis=1).astype(jnp.bfloat16)
    summed = lax.psum_scatter(
        jnp.concatenate(
            [
                lax.dot_general(
                    slot_rows, grad_gate_pre, slot_contract, preferred_element_type=jnp.float32
                ),
                lax.dot_general(
                    slot_rows, grad_up_pre, slot_contract, preferred_element_type=jnp.float32
                ),
                lax.dot_general(
                    slot_grads, hidden_act, slot_contract, preferred_element_type=jnp.float32
                ),
            ],
            axis=1,
        ).astype(jnp.bfloat16),
        "dp",
        scatter_dimension=0,
        tiled=True,
    ).astype(jnp.float32)
    grad_gate = summed[:, :hidden].astype(jnp.bfloat16)[None]
    grad_up = summed[:, hidden : 2 * hidden].astype(jnp.bfloat16)[None]
    grad_down = summed[:, 2 * hidden :].T.astype(jnp.bfloat16)[None]
    return (grad_tokens, grad_gate, grad_up, grad_down)


def solution(mesh):
    in_specs = (
        P(("dp", "expert"), None),
        P(("dp", "expert"), None),
        P(("dp", "expert"), None),
        P(("dp", "expert"), None),
        P("expert", "dp", None, None, None),
        P("expert", "dp", None),
        P("expert", "dp", None),
        P("expert", None, "dp"),
    )
    out_specs = (
        P(("dp", "expert"), None),
        P("expert", "dp", None),
        P("expert", "dp", None),
        P("expert", None, "dp"),
    )
    return jax.shard_map(shards, mesh=mesh, in_specs=in_specs, out_specs=out_specs, check_vma=False)
```

profile of v0, /device:TPU:2, one launch (start us, length us, event | category | flops | bytes accessed | tf_op | source)
XLA Modules:
  0.0 418.3 jit_solution(2112180043806233097)
XLA Ops:
  7.2 0.0 copy-start
  7.2 0.9 copy.14
  8.0 0.1 eq.29
  8.2 0.1 eq.25
  8.3 0.7 broadcast_multiply_fusion
  9.0 1.7 reduce-window.6
  10.8 0.3 slice_reduce_fusion
  11.1 0.1 copy.13
  11.2 0.1 mul.56
  11.3 0.1 fusion.8
  11.5 3.4 scatter_custom_fusion.1
  14.9 0.0 copy-done
  14.9 4.9 %gather_fusion = bf16[832,2048]{1,0:T(8,128)(2,1)} fusion(bf16[128,2048]{1,0:T(8,128)(2,1)S(1)} %copy-done, s32[1024]{0:T(1024)S(1)} %pad_clamp_fusion.1), kind=kCustom, calls=%fused_computation | custom fusion | bytes 6819072 | tf_op jit(solution)/shard_map/gather | solution.py:25
  19.8 5.9 %reshape.100 = f32[32,26,2048]{2,1,0:T(8,128)} reshape(bf16[832,2048]{1,0:T(8,128)(2,1)} %gather_fusion) | data formatting | bytes 10223616 | tf_op jit(solution)/shard_map/convert_element_type | solution.py:25
  25.7 0.0 copy-done.9
  25.7 0.1 copy.17
  25.8 0.1 reshape.130
  25.9 3.4 scatter_custom_fusion
  29.3 0.1 mul.58
  29.4 5.8 %multiply_convert_fusion = bf16[32,26,2048]{2,1,0:T(8,128)(2,1)} fusion(f32[32,26,2048]{2,1,0:T(8,128)} %reshape.100, f32[32,26]{1,0:T(8,128)S(1)} %mul.58), kind=kLoop, calls=%fused_computation.7 | loop fusion | flops 3407872 | bytes 10226944 | tf_op jit(solution)/shard_map/convert_element_type | solution.py:25
  35.3 11.8 %all-to-all-start = ((bf16[32,26,2048]{2,1,0:T(8,128)(2,1)}), bf16[32,26,2048]{2,1,0:T(8,128)(2,1)}, u32[]{:S(2)}, u32[]{:S(2)}) async-start(bf16[32,26,2048]{2,1,0:T(8,128)(2,1)} %multiply_convert_fusion), calls=%async_computation | async-start | bytes 8388608 | tf_op jit(solution)/shard_map/all_to_all | solution.py:32
  47.1 0.0 all-gather.4.cloned.1.call-start
  47.1 0.7 all-gather.4.cloned.1.call-update
  47.8 0.0 copy-done.2
  47.8 4.9 %gather_fusion.2 = bf16[832,2048]{1,0:T(8,128)(2,1)} fusion(bf16[128,2048]{1,0:T(8,128)(2,1)S(1)} %copy-done.2, s32[1024]{0:T(1024)S(1)} %pad_clamp_fusion.1), kind=kCustom, calls=%fused_computation.2 | custom fusion | bytes 6819072 | tf_op jit(solution)/shard_map/gather | solution.py:24
  52.7 4.9 %gather.14 = bf16[32,26,2048]{2,1,0:T(8,128)(2,1)} reshape(bf16[832,2048]{1,0:T(8,128)(2,1)} %gather_fusion.2) | data formatting | bytes 6815744 | tf_op jit(solution)/shard_map/gather | solution.py:24
  57.6 3.4 scatter_custom_fusion.2
  61.0 0.1 broadcast_in_dim.47
  61.1 4.8 %broadcast_select_fusion = bf16[32,26,2048]{2,1,0:T(8,128)(2,1)} fusion(bf16[32,26,2048]{2,1,0:T(8,128)(2,1)} %gather.14, pred[32,26]{1,0:T(8,128)(4,1)S(1)} %broadcast_in_dim.47), kind=kLoop, calls=%fused_computation.9 | loop fusion | flops 1703936 | bytes 6816576 | tf_op jit(solution)/shard_map/jit(_where)/select_n | solution.py:24
  65.8 75.0 %all-to-all-done = bf16[32,26,2048]{2,1,0:T(8,128)(2,1)} async-done(((bf16[32,26,2048]{2,1,0:T(8,128)(2,1)}), bf16[32,26,2048]{2,1,0:T(8,128)(2,1)}, u32[]{:S(2)}, u32[]{:S(2)}) %all-to-all-start) | async-done | bytes 3407904 | tf_op jit(solution)/shard_map/all_to_all | solution.py:32
  140.9 7.4 %all-to-all-start.2 = ((bf16[32,26,2048]{2,1,0:T(8,128)(2,1)}), bf16[32,26,2048]{2,1,0:T(8,128)(2,1)}, u32[]{:S(2)}, u32[]{:S(2)}) async-start(bf16[32,26,2048]{2,1,0:T(8,128)(2,1)} %broadcast_select_fusion), calls=%async_computation.2 | async-start | bytes 8388608 | tf_op jit(solution)/shard_map/all_to_all | solution.py:31
  148.3 0.0 all-gather.6.cloned.1.call-start
  148.4 0.7 all-gather.6.cloned.1.call-update
  149.1 0.0 all-gather.8.cloned.1.call-start
  149.1 0.7 all-gather.8.cloned.1.call-update
  149.8 0.2 reduce-scatter.2.cloned.1.call-start
  150.0 0.0 copy-done.6
  150.1 3.4 copy.18
  153.4 5.4 %reshape.101 = f32[832,1408]{1,0:T(8,128)} reshape(f32[1,1,32,26,1408]{4,3,2,1,0:T(8,128)} %copy.18) | data formatting | bytes 9371648 | tf_op jit(solution)/shard_map/convert_element_type | solution.py:42
  158.8 4.8 %fusion.21 = (f32[832,704]{1,0:T(8,128)}, f32[832,704]{1,0:T(8,128)S(1)}) fusion(f32[832,1408]{1,0:T(8,128)} %reshape.101), kind=kLoop, calls=%fused_computation.55 | loop fusion | bytes 9371648 | tf_op jit(solution)/shard_map/slice | solution.py:44
  163.6 3.3 copy.21
  166.9 2.1 copy.22
  169.0 3.3 reshape.95
  172.4 72.8 %all-to-all-done.2 = bf16[32,26,2048]{2,1,0:T(8,128)(2,1)} async-done(((bf16[32,26,2048]{2,1,0:T(8,128)(2,1)}), bf16[32,26,2048]{2,1,0:T(8,128)(2,1)}, u32[]{:S(2)}, u32[]{:S(2)}) %all-to-all-start.2) | async-done | bytes 3407904 | tf_op jit(solution)/shard_map/all_to_all | solution.py:31
  245.2 4.9 %reshape.99 = bf16[832,2048]{1,0:T(8,128)(2,1)} reshape(bf16[32,26,2048]{2,1,0:T(8,128)(2,1)} %all-to-all-done.2) | data formatting | bytes 6815744 | tf_op jit(solution)/shard_map/reshape | solution.py:34
  250.0 7.2 %multiply_convert_fusion.2 = (bf16[832,704]{0,1:T(8,128)(2,1)S(1)}, bf16[832,704]{0,1:T(8,128)(2,1)S(1)}) fusion(f32[832,704]{0,1:T(8,128)} %copy.22, f32[832,704]{0,1:T(8,128)} %copy.21, bf16[832,2048]{1,0:T(8,128)(2,1)S(1)} %reshape.95, bf16[1,704,2048]{2,1,0:T(8,128)(2,1)} %all-gather.4.cloned.1.call-done), kind=kOutput, calls=%fused_computation.19 | convolution fusion | flops 2406756352 | bytes 13320192 | tf_op jit(solution)/shard_map/dot_general | solution.py:49
  257.3 0.0 copy-start.10
  257.3 3.4 convolution_convert_fusion.1
  260.7 3.4 convolution_convert_fusion.2
  264.1 3.4 convolution_convert_fusion
  267.5 4.2 %pad_maximum_fusion = bf16[2048,2112]{0,1:T(8,128)(2,1)} fusion(bf16[2048,704]{0,1:T(8,128)(2,1)S(1)} %convolution_convert_fusion, bf16[2048,704]{0,1:T(8,128)(2,1)S(1)} %convolution_convert_fusion.1, bf16[2048,704]{0,1:T(8,128)(2,1)S(1)} %convolution_convert_fusion.2), kind=kLoop, calls=%fused_computation.6 | loop fusion | flops 25952256 | bytes 17301504 | tf_op jit(solution)/shard_map/concatenate | solution.py:66
  271.7 0.0 reduce-scatter.2.cloned.1.call-update
  271.7 0.0 all-gather.6.cloned.1.call-done
  271.8 1.2 copy-done.8
  273.0 7.7 %fusion.1 = f32[832,2048]{1,0:T(8,128)} fusion(bf16[832,704]{0,1:T(8,128)(2,1)S(1)} %copy-done.8, bf16[1,2048,704]{1,2,0:T(8,128)(2,1)} %all-gather.6.cloned.1.call-done), kind=kOutput, calls=%fused_computation.14 | convolution fusion | flops 2399141888 | bytes 10870784 | tf_op jit(solution)/shard_map/dot_general | solution.py:56
  280.8 7.0 %add_convert_fusion = bf16[832,2048]{1,0:T(8,128)(2,1)S(1)} fusion(f32[832,2048]{1,0:T(8,128)} %fusion.1, bf16[832,704]{0,1:T(8,128)(2,1)} %copy-done.10, bf16[1,2048,704]{1,2,0:T(8,128)(2,1)} %all-gather.8.cloned.1.call-done), kind=kOutput, calls=%fused_computation.8 | convolution fusion | flops 2402549760 | bytes 14278656 | tf_op jit(solution)/shard_map/dot_general | solution.py:58
  287.8 2.8 reshape.96
  290.7 5.3 %all-to-all-start.1 = ((bf16[32,26,2048]{2,1,0:T(8,128)(2,1)}), bf16[32,26,2048]{2,1,0:T(8,128)(2,1)}, u32[]{:S(2)}, u32[]{:S(2)}) async-start(bf16[32,26,2048]{2,1,0:T(8,128)(2,1)} %reshape.96), calls=%async_computation.1 | async-start | bytes 8388608 | tf_op jit(solution)/shard_map/all_to_all | solution.py:61
  296.0 93.9 %all-to-all-done.1 = bf16[32,26,2048]{2,1,0:T(8,128)(2,1)} async-done(((bf16[32,26,2048]{2,1,0:T(8,128)(2,1)}), bf16[32,26,2048]{2,1,0:T(8,128)(2,1)}, u32[]{:S(2)}, u32[]{:S(2)}) %all-to-all-start.1) | async-done | bytes 3407904 | tf_op jit(solution)/shard_map/all_to_all | solution.py:61
  389.9 3.3 reshape.97
  393.3 4.3 %gather_fusion.1 = bf16[768,2048]{1,0:T(8,128)(2,1)} fusion(bf16[832,2048]{1,0:T(8,128)(2,1)S(1)} %reshape.97, s32[1024]{0:T(1024)S(1)} %pad_clamp_fusion), kind=kCustom, calls=%fused_computation.1 | custom fusion | bytes 6294528 | tf_op jit(solution)/shard_map/gather | solution.py:63
  397.6 6.3 %reshape.98 = bf16[128,6,2048]{2,1,0:T(8,128)(2,1)} reshape(bf16[768,2048]{1,0:T(8,128)(2,1)} %gather_fusion.1) | data formatting | bytes 6291456 | tf_op jit(solution)/shard_map/reshape | solution.py:63
  403.9 5.7 %reduce_sum.25 = bf16[128,2048]{1,0:T(8,128)(2,1)} reduce(bf16[128,6,2048]{2,1,0:T(8,128)(2,1)} %reshape.98, bf16[]{:T(256)} %constant.33.clone.1), dimensions={1}, to_apply=%region_5.6 | reduce | flops 1310720 | bytes 3670018 | tf_op jit(solution)/shard_map/reduce_sum | solution.py:64
  409.6 2.2 slice_bitcast_fusion
  (26 shorter events, 0.1 us)
Async XLA Ops:
  7.2 7.7 %copy-start = (bf16[128,2048]{1,0:T(8,128)(2,1)S(1)}, bf16[128,2048]{1,0:T(8,128)(2,1)}, u32[]{:S(2)}) copy-start(bf16[128,2048]{1,0:T(8,128)(2,1)} %param.9) | copy-start | bytes 1572868
  19.8 5.9 %copy-start.9 = (f32[128,6]{0,1:T(8,128)S(1)}, f32[128,6]{0,1:T(8,128)}, u32[]{:S(2)}) copy-start(f32[128,6]{0,1:T(8,128)} %param.11) | copy-start | bytes 9220
  35.3 12.5 %copy-start.2 = (bf16[128,2048]{1,0:T(8,128)(2,1)S(1)}, bf16[128,2048]{1,0:T(8,128)(2,1)}, u32[]{:S(2)}) copy-start(bf16[128,2048]{1,0:T(8,128)(2,1)} %param.8) | copy-start | bytes 1572868
  35.3 105.6 %all-to-all-start = ((bf16[32,26,2048]{2,1,0:T(8,128)(2,1)}), bf16[32,26,2048]{2,1,0:T(8,128)(2,1)}, u32[]{:S(2)}, u32[]{:S(2)}) async-start(bf16[32,26,2048]{2,1,0:T(8,128)(2,1)} %multiply_convert_fusion), calls=%async_computation | async-start | bytes 8388608 | tf_op jit(solution)/shard_map/all_to_all | solution.py:32
  47.1 203.0 %all-gather.4.cloned.1.call-start = ((), (), s32[]{:S(2)}) async-start(), calls=%async_computation.4 | async-start | bytes 3244032 | tf_op jit(solution)/shard_map/all_gather | solution.py:48
  65.8 84.2 %copy-start.6 = (bf16[1,1,32,26,1408]{4,2,3,1,0:T(8,128)(2,1)S(1)}, bf16[1,1,32,26,1408]{4,2,3,1,0:T(8,128)(2,1)}, u32[]{:S(2)}) copy-start(bf16[1,1,32,26,1408]{4,2,3,1,0:T(8,128)(2,1)} %param.12) | copy-start | bytes 7028740
  140.9 104.3 %all-to-all-start.2 = ((bf16[32,26,2048]{2,1,0:T(8,128)(2,1)}), bf16[32,26,2048]{2,1,0:T(8,128)(2,1)}, u32[]{:S(2)}, u32[]{:S(2)}) async-start(bf16[32,26,2048]{2,1,0:T(8,128)(2,1)} %broadcast_select_fusion), calls=%async_computation.2 | async-start | bytes 8388608 | tf_op jit(solution)/shard_map/all_to_all | solution.py:31
  148.3 123.4 %all-gather.6.cloned.1.call-start = ((), (), s32[]{:S(2)}) async-start(), calls=%async_computation.5 | async-start | bytes 3244032 | tf_op jit(solution)/shard_map/all_gather | solution.py:37
  149.1 131.7 %all-gather.8.cloned.1.call-start = ((), (), s32[]{:S(2)}) async-start(), calls=%async_computation.6 | async-start | bytes 3244032 | tf_op jit(solution)/shard_map/all_gather | solution.py:38
  149.8 259.8 %reduce-scatter.2.cloned.1.call-start = ((), (), s32[]{:S(2)}) async-start(), calls=%async_computation.7 | async-start | bytes 9732096 | tf_op jit(solution)/shard_map/reduce_scatter | solution.py:65
  250.0 7.3 %copy-start.3 = (bf16[832,2048]{1,0:T(8,128)(2,1)S(1)}, bf16[832,2048]{1,0:T(8,128)(2,1)}, u32[]{:S(2)}) copy-start(bf16[832,2048]{1,0:T(8,128)(2,1)} %reshape.99) | copy-start | bytes 10223620
  257.3 3.4 copy-start.10
  257.3 3.4 copy-start.7
  260.7 3.4 copy-start.4
  260.7 3.4 copy-start.5
  271.7 1.3 copy-start.8
  290.7 99.3 %all-to-all-start.1 = ((bf16[32,26,2048]{2,1,0:T(8,128)(2,1)}), bf16[32,26,2048]{2,1,0:T(8,128)(2,1)}, u32[]{:S(2)}, u32[]{:S(2)}) async-start(bf16[32,26,2048]{2,1,0:T(8,128)(2,1)} %reshape.96), calls=%async_computation.1 | async-start | bytes 8388608 | tf_op jit(solution)/shard_map/all_to_all | solution.py:61
  397.6 14.2 %copy-start.1 = (bf16[128,2048]{1,0:T(8,128)(2,1)S(1)}, bf16[128,2048]{1,0:T(8,128)(2,1)}, u32[]{:S(2)}) copy-start(bf16[128,2048]{1,0:T(8,128)(2,1)} %param.9) | copy-start | bytes 1572868
Sparse Core Ops, SparseCore 0:
  49.7 34.2 all-gather.3
  151.0 34.2 all-gather.5
  187.1 34.1 all-gather.7
  271.8 52.2 reduce-scatter.1
where the time goes:
time: 422 us; the launch traced here: 418 us
  waiting for transfers between devices  244 us (58%)
  local copies, waits for them, and re-layouts  80.2 us (19%)
  matrix products  32.2 us (8%)
  starting transfers between devices  24.9 us (6%)
  other arithmetic  23.1 us (5%)
  between operations  14.1 us (3%)
    all_to_all x1, waiting for transfers between devices, shards(): lax.all_to_all(slot_back, 'expert', split_axis=0, concat_axis=0, tiled=True)  93.9 us
    all_to_all x1, waiting for transfers between devices, shards(): lax.all_to_all(send_grads, 'expert', split_axis=0, concat_axis=0, tiled=T...  75 us
    all_to_all x1, waiting for transfers between devices, shards(): lax.all_to_all(send_rows, 'expert', split_axis=0, concat_axis=0, tiled=True)  72.8 us
    all_to_all x1, starting transfers between devices, shards(): lax.all_to_all(send_grads, 'expert', split_axis=0, concat_axis=0, tiled=T...  11.8 us
    gather x2, local copies, waits for them, and re-layouts, shards(): tokens[slot_token]  9.77 us
    convert_element_type x2, local copies, waits for them, and re-layouts, shards(): pre_act = saved_pre.reshape(-1, 2 * hidden).astype(jnp.float32)  8.76 us
  transfers between devices with their start and end apart: 7, of which 3 were waited for; matrix products, arithmetic and copies ran while one was open for 25% of the time, Pallas kernels for 0%

commit v1 on v0

v1 whole, which is shorter than its diff:
```python
import jax
import jax.numpy as jnp
from jax import lax
from jax.experimental import pallas as pl
from jax.experimental.pallas import tpu as pltpu
from jax.sharding import PartitionSpec as P

MESH = pl.DeviceIdType.MESH
NZ, NX = 8, 4
CAP = 26
BLK = 128
GRP = NZ * CAP
SLOTS = NX * GRP
CH = 256
VMEM = pl.BlockSpec(memory_space=pltpu.VMEM)


def nt(a, b):
    return lax.dot_general(a, b, (((1,), (1,)), ((), ())), preferred_element_type=jnp.float32)


def tn(a, b):
    return lax.dot_general(a, b, (((0,), (0,)), ((), ())), preferred_element_type=jnp.float32)


def nn(a, b):
    return jnp.dot(a, b, preferred_element_type=jnp.float32)


def place():
    r, e = lax.axis_index("dp"), lax.axis_index("expert")
    return r, e // NX, lax.rem(e, NX)


def enter(r, z, x):
    barrier = pltpu.get_barrier_semaphore()
    for dz in (1, NZ - 1):
        pl.semaphore_signal(barrier, inc=1, device_id=(r, lax.rem(z + dz, NZ) * NX + x), device_id_type=MESH)
    for dx in range(1, NX):
        pl.semaphore_signal(barrier, inc=1, device_id=(r, z * NX + lax.rem(x + dx, NX)), device_id_type=MESH)
    pl.semaphore_wait(barrier, NX + 1)


def build_picker(z, meta, pick, slot_gate):
    ids = meta[:, 0:8, :]
    gates = meta[:, 8:16, :]
    upper = (
        lax.broadcasted_iota(jnp.int32, (BLK, BLK), 0) < lax.broadcasted_iota(jnp.int32, (BLK, BLK), 1)
    ).astype(jnp.bfloat16)
    row = lax.broadcasted_iota(jnp.int32, (GRP, BLK), 0)
    base = lax.broadcasted_iota(jnp.int32, (NZ, BLK), 0) * CAP
    for xp in range(NX):
        same = ids == (z * NX + xp).astype(jnp.float32)
        named = jnp.sum(jnp.where(same, 1.0, 0.0), axis=1)
        gate = jnp.sum(jnp.where(same, gates, 0.0), axis=1)
        earlier = nn(named.astype(jnp.bfloat16), upper).astype(jnp.int32)
        key = jnp.where(named > 0.5, base + earlier, -1)
        total = jnp.zeros((GRP, BLK), jnp.float32)
        for zz in range(NZ):
            hit = row == key[zz : zz + 1, :]
            pick[xp * GRP : (xp + 1) * GRP, zz * BLK : (zz + 1) * BLK] = jnp.where(hit, 1.0, 0.0).astype(jnp.bfloat16)
            total = total + jnp.where(hit, gate[zz : zz + 1, :], 0.0)
        slot_gate[xp * GRP : (xp + 1) * GRP, :] = jnp.sum(total, axis=1, keepdims=True)


def dispatch_kernel(
    cot, tok, own_meta, slot, pick, ag, meta, stage, slot_gate, z_send, z_recv, m_send, m_recv, x_send, x_recv
):
    r, z, x = place()
    half_chunks = cot.shape[1] // CH
    chunks = 2 * half_chunks
    enter(r, z, x)
    sides = ((1, (r, lax.rem(z + 1, NZ) * NX + x)), (NZ - 1, (r, lax.rem(z + NZ - 1, NZ) * NX + x)))
    mine = pl.ds(pl.multiple_of(z * BLK, BLK), BLK)
    meta[z] = own_meta[...]
    for j in range(half_chunks):
        ag[j, mine, :] = cot[:, j * CH : (j + 1) * CH]
        ag[half_chunks + j, mine, :] = tok[:, j * CH : (j + 1) * CH]

    def ring(i, j, s, dist):
        back, to = sides[i]
        origin = lax.rem(z + dist * (NZ - back), NZ)
        if s == 3:
            rows = pl.ds(pl.multiple_of(origin * BLK + i * (BLK // 2), BLK // 2), BLK // 2)
        else:
            rows = pl.ds(pl.multiple_of(origin * BLK, BLK), BLK)
        view = ag.at[j, rows, :]
        return pltpu.make_async_remote_copy(
            src_ref=view, dst_ref=view, send_sem=z_send.at[i, j, s], recv_sem=z_recv.at[i, j, s],
            device_id=to, device_id_type=MESH,
        )

    def ring_meta(i, s, dist):
        back, to = sides[i]
        origin = lax.rem(z + dist * (NZ - back), NZ)
        view = meta.at[origin, i * 8 : i * 8 + 8, :] if s == 3 else meta.at[origin]
        return pltpu.make_async_remote_copy(
            src_ref=view, dst_ref=view, send_sem=m_send.at[i, s], recv_sem=m_recv.at[i, s],
            device_id=to, device_id_type=MESH,
        )

    def exchange(j, d):
        to = lax.rem(x + d, NX)
        return pltpu.make_async_remote_copy(
            src_ref=stage.at[j, pl.ds(pl.multiple_of(to * GRP, 16), GRP), :],
            dst_ref=slot.at[j, pl.ds(pl.multiple_of(x * GRP, 16), GRP), :],
            send_sem=x_send.at[j, d - 1], recv_sem=x_recv.at[j, d - 1],
            device_id=(r, z * NX + to), device_id_type=MESH,
        )

    def arrival(j, d):
        src = lax.rem(x + NX - d, NX)
        view = slot.at[j, pl.ds(pl.multiple_of(src * GRP, 16), GRP), :]
        return pltpu.make_async_remote_copy(
            src_ref=view, dst_ref=view, send_sem=x_send.at[j, d - 1], recv_sem=x_recv.at[j, d - 1],
            device_id=(r, z * NX + src), device_id_type=MESH,
        )

    def tick(t, carry):
        for s in (4, 3, 2, 1, 0):
            j = t - s

            @pl.when((j >= 0) & (j < chunks))
            def _():
                if s > 0:

                    @pl.when(j == 0)
                    def _():
                        for i in range(2):
                            ring_meta(i, s - 1, s).wait_recv()
                            if s < 4:
                                ring_meta(i, s, s).start()

                    for i in range(2):
                        ring(i, j, s - 1, s).wait_recv()
                        if s < 4:
                            ring(i, j, s, s).start()
                else:

                    @pl.when(j == 0)
                    def _():
                        for i in range(2):
                            ring_meta(i, 0, 0).start()

                    for i in range(2):
                        ring(i, j, 0, 0).start()

        j = t - 4

        @pl.when(j == 0)
        def _():
            build_picker(z, meta, pick, slot_gate)

        @pl.when(j >= 0)
        def _():
            plain = (j >= half_chunks).astype(jnp.float32)
            for d in (2, 1, 3, 0):
                to = lax.rem(x + d, NX)
                rows = pl.ds(pl.multiple_of(to * GRP, 16), GRP)
                gate = slot_gate[rows, :]
                value = nn(pick[rows, :], ag[j])
                value = (value * (gate * (1.0 - plain) + plain)).astype(jnp.bfloat16)
                if d == 0:
                    slot[j, rows, :] = value
                else:
                    stage[j, rows, :] = value
                    exchange(j, d).start()

        return carry

    lax.fori_loop(0, chunks + 4, tick, 0)
    for i in range(2):
        for s in range(4):
            ring_meta(i, s, s).wait_send()

    def finish(j, carry):
        for i in range(2):
            for s in range(4):
                ring(i, j, s, s).wait_send()
        for d in (2, 1, 3):
            exchange(j, d).wait_send()
            arrival(j, d).wait_recv()
        return carry

    lax.fori_loop(0, chunks, finish, 0)


def middle_kernel(slot, pre, w_gate, w_up, w_down, back, p_gate, p_up, p_down, gh, g_gate, g_up, hidden_t):
    hidden = w_gate.shape[2]
    chunks = w_gate.shape[0]
    for g in range(NX):
        rows = slice(g * GRP, (g + 1) * GRP)
        gh[rows, :] = jnp.zeros((GRP, hidden), jnp.float32)

    def down(j, carry):
        for g in range(NX):
            rows = slice(g * GRP, (g + 1) * GRP)
            gh[rows, :] += nt(slot[j, rows, :], w_down[j])
        return carry

    lax.fori_loop(0, chunks, down, 0)
    acts = []
    for g in range(NX):
        rows = slice(g * GRP, (g + 1) * GRP)
        gate = pre[rows, :hidden].astype(jnp.float32)
        up = pre[rows, hidden:].astype(jnp.float32)
        sig = 1.0 / (1.0 + jnp.exp(-gate))
        grad = gh[rows, :]
        g_gate[rows, :] = (grad * up * sig * (1.0 + gate * (1.0 - sig))).astype(jnp.bfloat16)
        g_up[rows, :] = (grad * gate * sig).astype(jnp.bfloat16)
        acts.append((gate * sig * up).astype(jnp.bfloat16))
    hidden_t[...] = jnp.concatenate(acts, axis=0).T

    def rest(j, carry):
        for g in range(NX):
            rows = slice(g * GRP, (g + 1) * GRP)
            back[j, rows, :] = (nt(g_gate[rows, :], w_gate[j]) + nt(g_up[rows, :], w_up[j])).astype(jnp.bfloat16)
        p_gate[j] = tn(slot[chunks + j], g_gate[...]).astype(jnp.bfloat16)
        p_up[j] = tn(slot[chunks + j], g_up[...]).astype(jnp.bfloat16)
        p_down[j] = nn(hidden_t[...], slot[j]).astype(jnp.bfloat16)
        return carry

    lax.fori_loop(0, chunks, rest, 0)


def combine_kernel(back, pick, out, landed, part, z_out, z_in, z_send, z_recv, x_send, x_recv):
    r, z, x = place()
    chunks = back.shape[0]
    enter(r, z, x)
    sides = ((1, (r, lax.rem(z + 1, NZ) * NX + x)), (NZ - 1, (r, lax.rem(z + NZ - 1, NZ) * NX + x)))

    def exchange(j, d):
        to = lax.rem(x + d, NX)
        return pltpu.make_async_remote_copy(
            src_ref=back.at[j, pl.ds(pl.multiple_of(to * GRP, 16), GRP), :],
            dst_ref=landed.at[j, pl.ds(pl.multiple_of(x * GRP, 16), GRP), :],
            send_sem=x_send.at[j, d - 1], recv_sem=x_recv.at[j, d - 1],
            device_id=(r, z * NX + to), device_id_type=MESH,
        )

    def arrival(j, d):
        src = lax.rem(x + NX - d, NX)
        view = landed.at[j, pl.ds(pl.multiple_of(src * GRP, 16), GRP), :]
        return pltpu.make_async_remote_copy(
            src_ref=view, dst_ref=view, send_sem=x_send.at[j, d - 1], recv_sem=x_recv.at[j, d - 1],
            device_id=(r, z * NX + src), device_id_type=MESH,
        )

    def ring(i, j, s):
        to = sides[i][1]
        rows = pl.ds(0, BLK // 2) if s == 0 else pl.ds(0, BLK)
        return pltpu.make_async_remote_copy(
            src_ref=z_out.at[i, j, s, rows, :], dst_ref=z_in.at[i, j, s, rows, :],
            send_sem=z_send.at[i, j, s], recv_sem=z_recv.at[i, j, s], device_id=to, device_id_type=MESH,
        )

    def start(j, carry):
        for d in (2, 1, 3):
            exchange(j, d).start()
        own = pl.ds(pl.multiple_of(x * GRP, 16), GRP)
        landed[j, own, :] = back[j, own, :]
        return carry

    lax.fori_loop(0, chunks, start, 0)

    def tick(t, carry):
        for s in (4, 3, 2, 1):
            j = t - s

            @pl.when((j >= 0) & (j < chunks))
            def _():
                if s == 4:
                    for i in range(2):
                        ring(i, j, 3).wait_recv()
                    mine = pl.ds(pl.multiple_of(z * BLK, BLK), BLK)
                    total = part[j, mine, :] + z_in[0, j, 3].astype(jnp.float32) + z_in[1, j, 3].astype(jnp.float32)
                    out[j] = total.astype(jnp.bfloat16)
                else:
                    for i in range(2):
                        step = sides[i][0]
                        dest = lax.rem(z + step * (4 - s), NZ)
                        ring(i, j, s - 1).wait_recv()
                        if s == 1:
                            h = BLK // 2
                            for k in range(2):
                                value = part[j, pl.ds(pl.multiple_of(dest * BLK + k * h, h), h), :]
                                if k == i:
                                    value = value + z_in[i, j, 0, 0:h, :].astype(jnp.float32)
                                z_out[i, j, 1, k * h : (k + 1) * h, :] = value.astype(jnp.bfloat16)
                        else:
                            value = part[j, pl.ds(pl.multiple_of(dest * BLK, BLK), BLK), :]
                            z_out[i, j, s] = (value + z_in[i, j, s - 1].astype(jnp.float32)).astype(jnp.bfloat16)
                        ring(i, j, s).start()

        @pl.when(t < chunks)
        def _():
            for d in (2, 1, 3):
                arrival(t, d).wait_recv()
            part[t] = tn(pick[...], landed[t])
            h = BLK // 2
            dest = lax.rem(z + 4, NZ)
            for i in range(2):
                z_out[i, t, 0, 0:h, :] = part[t, pl.ds(pl.multiple_of(dest * BLK + i * h, h), h), :].astype(jnp.bfloat16)
                ring(i, t, 0).start()

        return carry

    lax.fori_loop(0, chunks + 4, tick, 0)

    def finish(j, carry):
        for i in range(2):
            for s in range(4):
                ring(i, j, s).wait_send()
        for d in (2, 1, 3):
            exchange(j, d).wait_send()
        return carry

    lax.fori_loop(0, chunks, finish, 0)


def shards(tokens, cotangent, expert_ids, gate_values, saved_pre, w_gate, w_up, w_down):
    width = tokens.shape[1]
    hidden = w_gate.shape[2]
    chunks = width // CH
    dma = pltpu.SemaphoreType.DMA
    bf = jnp.bfloat16
    gate_full = lax.all_gather(w_gate[0], "dp", axis=0)
    up_full = lax.all_gather(w_up[0], "dp", axis=0)
    down_full = lax.all_gather(w_down[0], "dp", axis=0)
    meta = jnp.concatenate(
        [
            jnp.pad(expert_ids.astype(jnp.float32).T, ((0, 2), (0, 0)), constant_values=-1.0),
            jnp.pad(gate_values.T, ((0, 2), (0, 0))),
        ],
        axis=0,
    )
    pre = saved_pre.reshape(NZ, NX, CAP, 2 * hidden).transpose(1, 0, 2, 3).reshape(SLOTS, 2 * hidden)
    slot, pick = pl.pallas_call(
        dispatch_kernel,
        out_shape=(
            jax.ShapeDtypeStruct((2 * chunks, SLOTS, CH), bf),
            jax.ShapeDtypeStruct((SLOTS, NZ * BLK), bf),
        ),
        in_specs=[VMEM] * 3,
        out_specs=(VMEM, VMEM),
        scratch_shapes=[
            pltpu.VMEM((2 * chunks, NZ * BLK, CH), bf),
            pltpu.VMEM((NZ, 16, BLK), jnp.float32),
            pltpu.VMEM((2 * chunks, SLOTS, CH), bf),
            pltpu.VMEM((SLOTS, 1), jnp.float32),
            dma((2, 2 * chunks, 4)),
            dma((2, 2 * chunks, 4)),
            dma((2, 4)),
            dma((2, 4)),
            dma((2 * chunks, 3)),
            dma((2 * chunks, 3)),
        ],
        compiler_params=pltpu.CompilerParams(
            collective_id=0, has_side_effects=True, vmem_limit_bytes=40 * 2**20
        ),
        cost_estimate=pl.CostEstimate(flops=7 * 10**9, bytes_accessed=10 * 2**20, transcendentals=0),
        name="dispatch",
    )(cotangent, tokens, meta)
    back, p_gate, p_up, p_down = pl.pallas_call(
        middle_kernel,
        out_shape=(
            jax.ShapeDtypeStruct((chunks, SLOTS, CH), bf),
            jax.ShapeDtypeStruct((chunks, CH, hidden), bf),
            jax.ShapeDtypeStruct((chunks, CH, hidden), bf),
            jax.ShapeDtypeStruct((chunks, hidden, CH), bf),
        ),
        in_specs=[VMEM] * 5,
        out_specs=(VMEM,) * 4,
        scratch_shapes=[
            pltpu.VMEM((SLOTS, hidden), jnp.float32),
            pltpu.VMEM((SLOTS, hidden), bf),
            pltpu.VMEM((SLOTS, hidden), bf),
            pltpu.VMEM((hidden, SLOTS), bf),
        ],
        compiler_params=pltpu.CompilerParams(vmem_limit_bytes=56 * 2**20),
        cost_estimate=pl.CostEstimate(flops=15 * 10**9, bytes_accessed=30 * 2**20, transcendentals=10**6),
        name="middle",
    )(slot, pre, gate_full, up_full, down_full)
    out = pl.pallas_call(
        combine_kernel,
        out_shape=jax.ShapeDtypeStruct((chunks, BLK, CH), bf),
        in_specs=[VMEM] * 2,
        out_specs=VMEM,
        scratch_shapes=[
            pltpu.VMEM((chunks, SLOTS, CH), bf),
            pltpu.VMEM((chunks, NZ * BLK, CH), jnp.float32),
            pltpu.VMEM((2, chunks, 4, BLK, CH), bf),
            pltpu.VMEM((2, chunks, 4, BLK, CH), bf),
            dma((2, chunks, 4)),
            dma((2, chunks, 4)),
            dma((chunks, 3)),
            dma((chunks, 3)),
        ],
        compiler_params=pltpu.CompilerParams(
            collective_id=1, has_side_effects=True, vmem_limit_bytes=40 * 2**20
        ),
        cost_estimate=pl.CostEstimate(flops=4 * 10**9, bytes_accessed=6 * 2**20, transcendentals=0),
        name="combine",
    )(back, pick)
    grad_tokens = out.transpose(1, 0, 2).reshape(BLK, width)
    grads = [
        lax.psum_scatter(p, "dp", scatter_dimension=0, tiled=True) for p in (p_gate, p_up, p_down)
    ]
    return (grad_tokens, *grads)


def solution(mesh):
    tok = P(("dp", "expert"), None)
    row = P("expert", "dp", None)
    col = P("expert", None, "dp")
    return jax.shard_map(
        shards,
        mesh=mesh,
        in_specs=(tok, tok, tok, tok, P("expert", "dp", None, None, None), row, row, col),
        out_specs=(tok, row, row, col),
        check_vma=False,
    )
```

time: 422 us -> 301 us (0.71)
  Pallas kernels: 0 us -> 206 us
  waiting for transfers between devices: 244 us -> 49.7 us
  local copies, waits for them, and re-layouts: 80.2 us -> 29.9 us
  matrix products: 32.2 us -> 0 us
  starting transfers between devices: 24.9 us -> 0.23 us
  other arithmetic: 23.1 us -> 0.01 us
    all_to_all x3 -> x0, waiting for transfers between devices: 242 us -> none  [the longest x1 93.9 us: shards(): lax.all_to_all(slot_back, 'expert', split_axis=0, concat_axis=0, tiled=True)]
    pallas_call x0 -> x3, Pallas kernels: none -> 206 us  [the longest x1 109 us: shards(): pl.pallas_call(dispatch_kernel, out_shape=(jax.ShapeDtypeStruct((2 * chun...]
    reduce_scatter x1 -> x3, waiting for transfers between devices: 0.01 us -> 46.6 us  [shards(): lax.psum_scatter(p, 'dp', scatter_dimension=0, tiled=True)]
    dot_general x6 -> x0, matrix products: 32.2 us -> none  [the longest x1 7.75 us: shards(): lax.dot_general(grad_gate_pre, gate_full, row_contract, preferred_element...]
    all_to_all x3 -> x0, starting transfers between devices: 24.6 us -> none  [the longest x1 11.8 us: shards(): lax.all_to_all(send_grads, 'expert', split_axis=0, concat_axis=0, tiled=T...]
    gather x4 -> x0, local copies, waits for them, and re-layouts: 19 us -> none  [the longest x2 9.77 us: shards(): tokens[slot_token]]
    convert_element_type x3 -> x0, local copies, waits for them, and re-layouts: 14.6 us -> none  [the longest x2 8.76 us: shards(): pre_act = saved_pre.reshape(-1, 2 * hidden).astype(jnp.float32)]
    scatter x3 -> x0, local copies, waits for them, and re-layouts: 10.1 us -> none  [the longest x1 3.38 us: shards(): jnp.zeros((experts * capacity,), jnp.int32).at[target].set(source_row)]
  transfers between devices with their start and end apart: 7 -> 6, of which waited for: 3 -> 2; matrix products, arithmetic and copies ran while one was open for 25% -> 8% of each run, Pallas kernels for 0% -> 57%
where the time goes in v1:
time: 301 us; the launch traced here: 300 us
  Pallas kernels  206 us (68%)
  waiting for transfers between devices  49.7 us (17%)
  local copies, waits for them, and re-layouts  29.9 us (10%)
  between operations  14.2 us (5%)
    pallas_call x1, Pallas kernels, shards(): pl.pallas_call(dispatch_kernel, out_shape=(jax.ShapeDtypeStruct((2 * chun...  109 us
    pallas_call x1, Pallas kernels, shards(): pl.pallas_call(combine_kernel, out_shape=jax.ShapeDtypeStruct((chunks, BL...  62 us
    reduce_scatter x3, waiting for transfers between devices, shards(): lax.psum_scatter(p, 'dp', scatter_dimension=0, tiled=True)  46.6 us
    pallas_call x1, Pallas kernels, shards(): pl.pallas_call(middle_kernel, out_shape=(jax.ShapeDtypeStruct((chunks, SL...  35 us
    reshape x3, local copies, waits for them, and re-layouts, shards(): saved_pre.reshape(NZ, NX, CAP, 2 * hidden).transpose(1, 0, 2, 3)  10.7 us
    unnamed x15, local copies, waits for them, and re-layouts  9.63 us
  transfers between devices with their start and end apart: 6, of which 2 were waited for; matrix products, arithmetic and copies ran while one was open for 8% of the time, Pallas kernels for 57%

profile of v1, /device:TPU:2, one launch (start us, length us, event | category | flops | bytes accessed | tf_op | source)
XLA Modules:
  0.0 300.1 jit_solution(5991613688878677854)
XLA Ops:
  7.2 0.0 all-gather.6.cloned.1.call-start
  7.2 0.7 all-gather.6.cloned.1.call-update
  7.9 0.0 all-gather.4.cloned.1.call-start
  7.9 0.7 all-gather.4.cloned.1.call-update
  8.6 0.0 all-gather.8.cloned.1.call-start
  8.7 0.7 all-gather.8.cloned.1.call-update
  9.4 0.0 reduce-scatter.4.cloned.1.call-start
  9.4 4.0 %reshape.17 = bf16[8,4,26,1408]{3,1,0,2:T(4,128)(2,1)S(1)} reshape(bf16[1,1,32,26,1408]{4,2,3,1,0:T(8,128)(2,1)} %param.12) | data formatting | bytes 4685824 | tf_op jit(solution)/shard_map/reshape | solution.py:337
  13.5 2.4 copy.32
  15.8 0.0 copy-start.4
  15.8 0.0 copy-start.5
  15.8 0.0 copy-start
  15.8 0.0 copy-start.1
  15.8 4.3 %reshape.18.pre = bf16[832,1408]{1,0:T(8,128)(2,1)} reshape(bf16[4,8,26,1408]{3,2,1,0:T(8,128)(2,1)} %bitcast.13) | data formatting | bytes 4685824 | tf_op jit(solution)/shard_map/reshape | solution.py:337
  20.2 0.0 copy-done.4
  20.2 0.0 copy-done.5
  20.2 0.0 copy-done
  20.2 0.0 copy-done.1
  20.2 109.0 %dispatch.1 = (bf16[16,832,256]{2,1,0:T(8,128)(2,1)S(1)}, bf16[832,1024]{1,0:T(8,128)(2,1)S(1)}) custom-call(bf16[128,2048]{1,0:T(8,128)(2,1)S(1)} %copy-done, bf16[128,2048]{1,0:T(8,128)(2,1)S(1)} %copy-done.1, f32[16,128]{1,0:T(8,128)S(1)} %select_maximum_fusion.own_meta), custom_call_target="tpu_custom_call" | custom-call | flops 7000000000 | bytes 10485760 | tf_op jit(solution)/shard_map/dispatch/pallas_call | solution.py:338
  129.3 0.0 copy-start.3
  129.3 2.8 copy-done.3
  132.1 0.0 all-gather.6.cloned.1.call-done
  132.1 4.6 %copy.26.w_up = bf16[8,256,704]{2,1,0:T(8,128)(2,1)} copy(bf16[8,256,704]{1,2,0:T(8,128)(2,1)} %all-gather.6.cloned.1.call-done) | data formatting | bytes 5767168 | tf_op jit(solution)/shard_map/all_gather | solution.py:328
  136.7 0.0 all-gather.4.cloned.1.call-done
  136.7 4.6 %copy.25.w_gate = bf16[8,256,704]{2,1,0:T(8,128)(2,1)} copy(bf16[8,256,704]{1,2,0:T(8,128)(2,1)} %all-gather.4.cloned.1.call-done) | data formatting | bytes 5767168 | tf_op jit(solution)/shard_map/all_gather | solution.py:327
  141.3 0.0 all-gather.8.cloned.1.call-done.w_down
  141.3 35.0 %middle.1 = (bf16[8,832,256]{2,1,0:T(8,128)(2,1)}, bf16[8,256,704]{2,1,0:T(8,128)(2,1)}, bf16[8,256,704]{2,1,0:T(8,128)(2,1)}, bf16[8,704,256]{2,1,0:T(8,128)(2,1)}) custom-call(bf16[16,832,256]{2,1,0:T(8,128)(2,1)} %copy-done.3, bf16[832,1408]{1,0:T(8,128)(2,1)} %reshape.18.pre, bf16[8,256,704]{2,1,0:T(8,128)(2,1)} %copy.25.w_gate, ...), custom_call_target="tpu_custom_call" | custom-call | flops 15000000512 | bytes 31457280 | tf_op jit(solution)/shard_map/middle/pallas_call | solution.py:364
  176.3 0.0 reduce-scatter.4.cloned.1.call-update
  176.3 0.0 reduce-scatter.6.cloned.1.call-start
  176.4 0.5 reduce-scatter.6.cloned.1.call-update
  176.9 0.0 reduce-scatter.8.cloned.1.call-start
  177.0 0.5 reduce-scatter.8.cloned.1.call-update
  177.5 0.0 copy-start.2
  177.5 2.0 copy-done.2
  179.5 62.0 %combine.1 = bf16[8,128,256]{2,1,0:T(8,128)(2,1)S(1)} custom-call(bf16[8,832,256]{2,1,0:T(8,128)(2,1)S(1)} %copy-done.2, bf16[832,1024]{1,0:T(8,128)(2,1)S(1)} %get-tuple-element.12.pick), custom_call_target="tpu_custom_call" | custom-call | flops 4000000000 | bytes 6291456 | tf_op jit(solution)/shard_map/combine/pallas_call | solution.py:384
  241.5 0.3 copy.27
  241.8 1.0 copy.28
  242.8 0.0 reduce-scatter.4.cloned.1.call-done
  242.8 1.9 copy.29
  244.7 9.0 %reduce-scatter.6.cloned.1.call-done = bf16[1,256,704]{2,1,0:T(8,128)(2,1)} async-done(((bf16[8,256,704]{2,1,0:T(8,128)(2,1)}), bf16[1,256,704]{2,1,0:T(8,128)(2,1)}) %reduce-scatter.6.cloned.1.call-update) | async-done | bytes 360464 | tf_op jit(solution)/shard_map/reduce_scatter | solution.py:407
  253.7 1.9 copy.30
  255.6 37.6 %reduce-scatter.8.cloned.1.call-done = bf16[1,704,256]{2,1,0:T(8,128)(2,1)} async-done(((bf16[8,704,256]{2,1,0:T(8,128)(2,1)}), bf16[1,704,256]{2,1,0:T(8,128)(2,1)}) %reduce-scatter.8.cloned.1.call-update) | async-done | bytes 360464 | tf_op jit(solution)/shard_map/reduce_scatter | solution.py:407
  (2 shorter events, 0.0 us)
Async XLA Ops:
  7.2 124.9 %all-gather.6.cloned.1.call-start = ((), (), s32[]{:S(2)}) async-start(), calls=%async_computation.4 | async-start | bytes 3244032 | tf_op jit(solution)/shard_map/all_gather | solution.py:328
  7.9 128.8 %all-gather.4.cloned.1.call-start = ((), (), s32[]{:S(2)}) async-start(), calls=%async_computation.3 | async-start | bytes 3244032 | tf_op jit(solution)/shard_map/all_gather | solution.py:327
  8.6 132.7 %all-gather.8.cloned.1.call-start = ((), (), s32[]{:S(2)}) async-start(), calls=%async_computation.5 | async-start | bytes 3244032 | tf_op jit(solution)/shard_map/all_gather | solution.py:329
  9.4 233.4 %reduce-scatter.4.cloned.1.call-start = ((), (), s32[]{:S(2)}) async-start(), calls=%async_computation.6 | async-start | bytes 3538944 | tf_op jit(solution)/shard_map/reduce_scatter | solution.py:407
  15.8 4.4 %copy-start.4 = (s32[128,6]{0,1:T(8,128)S(1)}, s32[128,6]{0,1:T(8,128)}, u32[]{:S(2)}) copy-start(s32[128,6]{0,1:T(8,128)} %param.10) | copy-start | bytes 9220
  15.8 4.4 %copy-start.5 = (f32[128,6]{0,1:T(8,128)S(1)}, f32[128,6]{0,1:T(8,128)}, u32[]{:S(2)}) copy-start(f32[128,6]{0,1:T(8,128)} %param.11) | copy-start | bytes 9220
  15.8 4.4 %copy-start = (bf16[128,2048]{1,0:T(8,128)(2,1)S(1)}, bf16[128,2048]{1,0:T(8,128)(2,1)}, u32[]{:S(2)}) copy-start(bf16[128,2048]{1,0:T(8,128)(2,1)} %cot.1) | copy-start | bytes 1572868
  15.8 4.4 %copy-start.1 = (bf16[128,2048]{1,0:T(8,128)(2,1)S(1)}, bf16[128,2048]{1,0:T(8,128)(2,1)}, u32[]{:S(2)}) copy-start(bf16[128,2048]{1,0:T(8,128)(2,1)} %tok.1) | copy-start | bytes 1572868
  129.3 2.8 copy-start.3
  176.3 77.4 %reduce-scatter.6.cloned.1.call-start = ((), (), s32[]{:S(2)}) async-start(), calls=%async_computation.7 | async-start | bytes 3538944 | tf_op jit(solution)/shard_map/reduce_scatter | solution.py:407
  176.9 116.3 %reduce-scatter.8.cloned.1.call-start = ((), (), s32[]{:S(2)}) async-start(), calls=%async_computation.8 | async-start | bytes 3244032 | tf_op jit(solution)/shard_map/reduce_scatter | solution.py:407
  177.5 2.0 copy-start.2
Sparse Core Ops, SparseCore 0:
  9.8 32.1 all-gather.5
  43.9 29.7 all-gather.3
  75.5 29.8 all-gather.7
  176.5 37.2 reduce-scatter.3
  216.2 37.5 reduce-scatter.5
  256.7 36.4 reduce-scatter.7

commit v2 on v0

v2 whole, which is shorter than its diff:
```python
import jax
import jax.numpy as jnp
from jax import lax
from jax.experimental import pallas as pl
from jax.experimental.pallas import tpu as pltpu
from jax.sharding import PartitionSpec as P

MESH = pl.DeviceIdType.MESH
NZ, NX, NY = 8, 4, 4
CAP = 26
BLK = 128
GRP = NZ * CAP
SLOTS = NX * GRP
CH = 256
VIA = 112
KEEP = 5
HALF = BLK // 2
BF = jnp.bfloat16
F32 = jnp.float32


def nt(a, b):
    return lax.dot_general(a, b, (((1,), (1,)), ((), ())), preferred_element_type=F32)


def tn(a, b):
    return lax.dot_general(a, b, (((0,), (0,)), ((), ())), preferred_element_type=F32)


def nn(a, b):
    return jnp.dot(a, b, preferred_element_type=F32)


def span(start, size, unit):
    return pl.ds(pl.multiple_of(start, unit), size)


def build_picker(z, meta, pick, slot_gate):
    ids = meta[:, 0:8, :]
    gates = meta[:, 8:16, :]
    upper = (
        lax.broadcasted_iota(jnp.int32, (BLK, BLK), 0) < lax.broadcasted_iota(jnp.int32, (BLK, BLK), 1)
    ).astype(BF)
    row = lax.broadcasted_iota(jnp.int32, (GRP, BLK), 0)
    base = lax.broadcasted_iota(jnp.int32, (NZ, BLK), 0) * CAP
    for xp in range(NX):
        same = ids == (z * NX + xp).astype(F32)
        named = jnp.sum(jnp.where(same, 1.0, 0.0), axis=1)
        gate = jnp.sum(jnp.where(same, gates, 0.0), axis=1)
        earlier = nn(named.astype(BF), upper).astype(jnp.int32)
        key = jnp.where(named > 0.5, base + earlier, -1)
        total = jnp.zeros((GRP, BLK), F32)
        for zz in range(NZ):
            hit = row == key[zz : zz + 1, :]
            pick[xp * GRP : (xp + 1) * GRP, zz * BLK : (zz + 1) * BLK] = jnp.where(hit, 1.0, 0.0).astype(BF)
            total = total + jnp.where(hit, gate[zz : zz + 1, :], 0.0)
        slot_gate[xp * GRP : (xp + 1) * GRP, :] = jnp.sum(total, axis=1, keepdims=True)


def kernel(
    cot, tok, own_meta, pre, w_gate, w_up, w_down, out, grad_gate, grad_up, grad_down,
    meta, ag, slot, stage, relay, pick, slot_gate, part, z_in, weights, gh, g_gate, g_up, hid, pre_in, pre32, tmp,
    sib_out, sib_in, y_out, y_half, y_full,
    z_send, z_recv, m_send, m_recv, x_send, x_recv, b_send, b_recv, w_send, w_recv, s_send, s_recv, y_send, y_recv, p_sem,
):
    r, e = lax.axis_index("dp"), lax.axis_index("expert")
    y, c = r // 2, lax.rem(r, 2)
    z, x = e // NX, lax.rem(e, NX)
    hidden = w_gate.shape[1]
    n = cot.shape[1] // CH

    def at(yy=y, cc=c, zz=z, xx=x):
        return (yy * 2 + cc, zz * NX + xx)

    z_to = (at(zz=lax.rem(z + 1, NZ)), at(zz=lax.rem(z + NZ - 1, NZ)))
    x_to = (at(xx=lax.rem(x + 1, NX)), at(xx=lax.rem(x + NX - 1, NX)))
    y_to = (at(yy=lax.rem(y + 1, NY)), at(yy=lax.rem(y + NY - 1, NY)))
    sibling = at(cc=1 - c)
    z_step = (1, NZ - 1)
    barrier = pltpu.get_barrier_semaphore()
    peers = (*z_to, *x_to, *y_to, sibling)
    for peer in peers:
        pl.semaphore_signal(barrier, inc=1, device_id=peer, device_id_type=MESH)
    pl.semaphore_wait(barrier, len(peers))

    def send(src, dst, s_sem, r_sem, to):
        return pltpu.make_async_remote_copy(
            src_ref=src, dst_ref=dst, send_sem=s_sem, recv_sem=r_sem, device_id=to, device_id_type=MESH
        )

    def block_of(k):
        q = k // 2
        off = 2 - q + 3 * (q // 2) - 2 * (q // 3)
        core = c + (1 - 2 * c) * (1 - lax.rem(k, 2))
        return lax.rem(y + off, NY) * 2 + core

    def w_copy(m, what):
        mine = y * 2 + c
        low = lax.rem(y + NY - 1, NY) * 2 + c
        high = lax.rem(y + 1, NY) * 2 + c
        far = lax.rem(y + 2, NY) * 2 + c
        h = CH // 2
        view, to = (
            (weights.at[m, mine], y_to[0]),
            (weights.at[m, mine], y_to[1]),
            (weights.at[m, low, 0:h, :], y_to[0]),
            (weights.at[m, high, h : 2 * h, :], y_to[1]),
            (weights.at[m, mine], sibling),
            (weights.at[m, low], sibling),
            (weights.at[m, high], sibling),
            (weights.at[m, far], sibling),
        )[what]
        return send(view, view, w_send.at[m, what], w_recv.at[m, what], to)

    def w_arrival(m, what):
        low = lax.rem(y + NY - 1, NY)
        high = lax.rem(y + 1, NY)
        far = lax.rem(y + 2, NY)
        h = CH // 2
        view, source = (
            (weights.at[m, low * 2 + c], y_to[1]),
            (weights.at[m, high * 2 + c], y_to[0]),
            (weights.at[m, far * 2 + c, 0:h, :], y_to[1]),
            (weights.at[m, far * 2 + c, h : 2 * h, :], y_to[0]),
            (weights.at[m, y * 2 + 1 - c], sibling),
            (weights.at[m, low * 2 + 1 - c], sibling),
            (weights.at[m, high * 2 + 1 - c], sibling),
            (weights.at[m, far * 2 + 1 - c], sibling),
        )[what]
        return send(view, view, w_send.at[m, what], w_recv.at[m, what], source)

    def w_start(m):
        for what in (0, 1, 4):
            w_copy(m, what).start()

    def w_forward(m):
        for i in range(2):
            w_arrival(m, i).wait_recv()
            w_copy(m, 2 + i).start()
            w_copy(m, 5 + i).start()

    def w_far(m):
        for i in range(2):
            w_arrival(m, 2 + i).wait_recv()
        w_copy(m, 7).start()

    def w_done(m):
        for what in range(4, 8):
            w_arrival(m, what).wait_recv()

    def ring(i, j, s, dist):
        origin = lax.rem(z + dist * (NZ - z_step[i]), NZ)
        rows = span(origin * BLK + i * HALF, HALF, HALF) if s == 3 else span(origin * BLK, BLK, BLK)
        view = ag.at[lax.rem(j, n), rows, :]
        return send(view, view, z_send.at[i, j, s], z_recv.at[i, j, s], z_to[i])

    def ring_meta(i, s, dist):
        origin = lax.rem(z + dist * (NZ - z_step[i]), NZ)
        view = meta.at[origin, i * 8 : i * 8 + 8, :] if s == 3 else meta.at[origin]
        return send(view, view, m_send.at[i, s], m_recv.at[i, s], z_to[i])

    def x_copy(j, what):
        i = what % 2
        st, sl, rl = lax.rem(j, 4), lax.rem(j, 2 * n), lax.rem(j, n)
        near = lax.rem(x + (1 if i == 0 else NX - 1), NX) * GRP
        far = lax.rem(x + 2, NX) * GRP
        other = lax.rem(x + (NX - 1 if i == 0 else 1), NX) * GRP
        lo, size = (0, VIA) if i == 0 else (VIA, GRP - VIA)
        if what < 2:
            src, dst = stage.at[st, span(near, GRP, 16), :], slot.at[sl, span(x * GRP, GRP, 16), :]
        elif what < 4:
            src, dst = stage.at[st, span(far + lo, size, 16), :], relay.at[rl, lo : lo + size, :]
        else:
            src, dst = relay.at[rl, lo : lo + size, :], slot.at[sl, span(other + lo, size, 16), :]
        return send(src, dst, x_send.at[j, what], x_recv.at[j, what], x_to[i])

    def x_arrival(j, what):
        i = what % 2
        sl, rl = lax.rem(j, 2 * n), lax.rem(j, n)
        other = lax.rem(x + (NX - 1 if i == 0 else 1), NX) * GRP
        far = lax.rem(x + 2, NX) * GRP
        lo, size = (0, VIA) if i == 0 else (VIA, GRP - VIA)
        if what < 2:
            view = slot.at[sl, span(other, GRP, 16), :]
        elif what < 4:
            view = relay.at[rl, lo : lo + size, :]
        else:
            view = slot.at[sl, span(far + lo, size, 16), :]
        return send(view, view, x_send.at[j, what], x_recv.at[j, what], x_to[1 - i])

    def back_out(i, k, s):
        return ag.at[k, (i * 4 + s) * BLK : (i * 4 + s) * BLK + (HALF if s == 0 else BLK), :]

    def back_ring(i, k, s):
        rows = slice(0, HALF if s == 0 else BLK)
        return send(back_out(i, k, s), z_in.at[i, k, s, rows, :], b_send.at[i, k, s], b_recv.at[i, k, s], z_to[i])

    def sib_copy(m, q):
        return send(sib_out.at[m], sib_in.at[m, q], s_send.at[m, q], s_recv.at[m, q], sibling)

    def y_copy(m, what):
        h = CH // 2
        src, dst, to = (
            (y_out.at[m, 0, 0:h, :], y_half.at[m, 0:h, :], y_to[0]),
            (y_out.at[m, 0, h : 2 * h, :], y_half.at[m, h : 2 * h, :], y_to[1]),
            (y_out.at[m, 1], y_full.at[m, 0], y_to[0]),
            (y_out.at[m, 0], y_full.at[m, 1], y_to[1]),
        )[what]
        return send(src, dst, y_send.at[m, what], y_recv.at[m, what], to)

    def reduce_block(m, k, chunk, act):
        q = k // 2
        h = CH // 2
        tmp[...] = tn(slot[chunk], act[...])

        @pl.when(lax.rem(k, 2) == 0)
        def _():
            @pl.when(q > 0)
            def _():
                sib_copy(m, q - 1).wait_send()

            sib_out[m] = tmp[...].astype(BF)
            sib_copy(m, q).start()

        @pl.when(lax.rem(k, 2) == 1)
        def _():
            sib_copy(m, q).wait_recv()
            tmp[...] += sib_in[m, q].astype(F32)

        @pl.when(k == 1)
        def _():
            y_out[m, 0] = tmp[...].astype(BF)
            y_copy(m, 0).start()
            y_copy(m, 1).start()

        @pl.when(k == 3)
        def _():
            y_copy(m, 0).wait_recv()
            tmp[0:h, :] += y_half[m, 0:h, :].astype(F32)
            y_out[m, 1] = tmp[...].astype(BF)
            y_copy(m, 2).start()

        @pl.when(k == 5)
        def _():
            y_copy(m, 0).wait_send()
            y_copy(m, 1).wait_send()
            y_copy(m, 1).wait_recv()
            tmp[h : 2 * h, :] += y_half[m, h : 2 * h, :].astype(F32)
            y_out[m, 0] = tmp[...].astype(BF)
            y_copy(m, 3).start()

        @pl.when(k == 7)
        def _():
            y_copy(m, 2).wait_recv()
            y_copy(m, 3).wait_recv()
            total = tmp[...] + y_full[m, 0].astype(F32) + y_full[m, 1].astype(F32)
            if m == 0:
                grad_down[...] = total.T.astype(BF)
            else:
                (grad_gate, grad_up)[m - 1][...] = total.astype(BF)

    def pre_copy(g):
        return pltpu.make_async_copy(pre.at[:, g], pre_in.at[g % 2], p_sem.at[g])

    def activations(g):
        pre_copy(g).wait()
        for zz in range(NZ):
            pre32[zz * CAP : (zz + 1) * CAP, :] = pre_in[g % 2, zz].astype(F32)
        if g + 2 < NX:
            pre_copy(g + 2).start()

        def rows16(b, carry):
            src = span(b * 16, 16, 16)
            dst = span(g * GRP + b * 16, 16, 16)
            gate, up = pre32[src, :hidden], pre32[src, hidden:]
            sig = 1.0 / (1.0 + jnp.exp(-gate))
            g_gate[dst, :] = (up * sig * (1.0 + gate * (1.0 - sig))).astype(BF)
            g_up[dst, :] = (gate * sig).astype(BF)
            hid[dst, :] = (gate * sig * up).astype(BF)
            return carry

        lax.fori_loop(0, GRP // 16, rows16, 0)
        gh[g * GRP : (g + 1) * GRP, :] = jnp.zeros((GRP, hidden), F32)

    pre_copy(0).start()
    pre_copy(1).start()
    mine = span(z * BLK, BLK, BLK)
    meta[z] = own_meta[...]
    own = y * 2 + c
    weights[0, own] = w_down[...].T
    w_start(0)
    weights[1, own] = w_gate[...]
    weights[2, own] = w_up[...]

    def tick(t, carry):
        for s in (4, 3, 2, 1, 0):
            j = t - s

            @pl.when((j >= 0) & (j < 2 * n))
            def _():
                if s > 0:

                    @pl.when(j == 0)
                    def _():
                        for i in range(2):
                            ring_meta(i, s - 1, s).wait_recv()
                            if s < 4:
                                ring_meta(i, s, s).start()

                    for i in range(2):
                        ring(i, j, s - 1, s).wait_recv()
                        if s < 4:
                            ring(i, j, s, s).start()
                else:

                    @pl.when(j == 0)
                    def _():
                        for i in range(2):
                            ring_meta(i, 0, 0).start()

                    columns = span(block_of(lax.rem(j, n)) * CH, CH, CH)

                    @pl.when(j < n)
                    def _():
                        ag[lax.rem(j, n), mine, :] = cot[:, columns]

                    @pl.when(j >= n)
                    def _():
                        ag[lax.rem(j, n), mine, :] = tok[:, columns]

                    for i in range(2):
                        ring(i, j, 0, 0).start()

        for s in (4, 3, 2, 1):
            k = t - (2 * n + 6) - s
            kp = lax.rem(k + KEEP, KEEP)

            @pl.when((k >= 0) & (k < n))
            def _():
                if s == 4:
                    for i in range(2):
                        back_ring(i, k, 3).wait_recv()
                    total = part[kp, mine, :] + z_in[0, k, 3].astype(F32) + z_in[1, k, 3].astype(F32)
                    out[:, span(block_of(k) * CH, CH, CH)] = total.astype(BF)
                else:
                    for i in range(2):
                        dest = lax.rem(z + z_step[i] * (4 - s), NZ)
                        back_ring(i, k, s - 1).wait_recv()
                        base = (i * 4 + s) * BLK
                        if s == 1:
                            for p in range(2):
                                value = part[kp, span(dest * BLK + p * HALF, HALF, HALF), :]
                                if p == i:
                                    value = value + z_in[i, k, 0, 0:HALF, :].astype(F32)
                                ag[k, base + p * HALF : base + (p + 1) * HALF, :] = value.astype(BF)
                        else:
                            value = part[kp, span(dest * BLK, BLK, BLK), :]
                            ag[k, base : base + BLK, :] = (value + z_in[i, k, s - 1].astype(F32)).astype(BF)
                        back_ring(i, k, s).start()

        jr = t - 5

        @pl.when((jr >= 0) & (jr < 3 * n))
        def _():
            for i in range(2):
                x_arrival(jr, 2 + i).wait_recv()
                x_copy(jr, 4 + i).start()

        @pl.when((jr >= 0) & (jr < 2 * n))
        def _():
            for i in range(2):
                for s in range(4):
                    ring(i, jr, s, s).wait_send()

        j = t - 4

        @pl.when(j == 0)
        def _():
            build_picker(z, meta, pick, slot_gate)

        @pl.when((j >= 4) & (j < 3 * n))
        def _():
            for what in range(4):
                x_copy(j - 4, what).wait_send()

        def put(d, rows, value):
            if d == 0:
                slot[lax.rem(j, 2 * n), rows, :] = value
            else:
                stage[lax.rem(j, 4), rows, :] = value
            for what in {2: (2, 3), 1: (0,), 3: (1,), 0: ()}[d]:
                x_copy(j, what).start()

        @pl.when((j >= 0) & (j < 2 * n))
        def _():
            plain = (j >= n).astype(F32)
            for d in (2, 1, 3, 0):
                rows = span(lax.rem(x + d, NX) * GRP, GRP, 16)
                value = nn(pick[rows, :], ag[lax.rem(j, n)])
                put(d, rows, (value * (slot_gate[rows, :] * (1.0 - plain) + plain)).astype(BF))

        @pl.when((j >= 2 * n) & (j < 3 * n))
        def _():
            block = block_of(j - 2 * n)
            for d in (2, 1, 3, 0):
                rows = span(lax.rem(x + d, NX) * GRP, GRP, 16)
                put(d, rows, (nt(g_gate[rows, :], weights[1, block]) + nt(g_up[rows, :], weights[2, block])).astype(BF))

        ja = t - 6

        @pl.when((ja >= 0) & (ja < 3 * n))
        def _():
            for what in (0, 1, 4, 5):
                x_arrival(ja, what).wait_recv()

        @pl.when((ja >= 1) & (ja < 3 * n + 1))
        def _():
            for what in (4, 5):
                x_copy(ja - 1, what).wait_send()

        for when, step in (
            (2, lambda: (w_forward(0), w_start(1))),
            (4, lambda: w_far(0)),
            (5, lambda: (w_done(0), w_forward(1), w_start(2))),
            (7, lambda: w_far(1)),
            (8, lambda: w_forward(2)),
            (9, lambda: w_done(1)),
            (10, lambda: w_far(2)),
            (12, lambda: w_done(2)),
        ):

            @pl.when(t == when)
            def _():
                step()

        for g in range(NX):

            @pl.when(t == g)
            def _():
                activations(g)

        @pl.when((ja >= 0) & (ja < n))
        def _():
            block = block_of(ja)
            for g in range(NX):
                rows = slice(g * GRP, (g + 1) * GRP)
                gh[rows, :] += nn(slot[ja, rows, :], weights[0, block])

        @pl.when(ja == n - 1)
        def _():
            for g in range(NX):
                rows = slice(g * GRP, (g + 1) * GRP)
                g_gate[rows, :] = (gh[rows, :] * g_gate[rows, :].astype(F32)).astype(BF)
                g_up[rows, :] = (gh[rows, :] * g_up[rows, :].astype(F32)).astype(BF)

        @pl.when((ja >= 1) & (ja < n + 1))
        def _():
            reduce_block(0, ja - 1, ja - 1, hid)

        @pl.when((ja >= n) & (ja < 2 * n))
        def _():
            reduce_block(1, ja - n, ja, g_gate)
            reduce_block(2, ja - n, ja, g_up)

        @pl.when((ja >= 2 * n) & (ja < 3 * n))
        def _():
            k = ja - 2 * n
            kp = lax.rem(k, KEEP)
            part[kp] = tn(pick[...], slot[k])
            dest = lax.rem(z + 4, NZ)
            for i in range(2):
                value = part[kp, span(dest * BLK + i * HALF, HALF, HALF), :]
                ag[k, i * 4 * BLK : i * 4 * BLK + HALF, :] = value.astype(BF)
                back_ring(i, k, 0).start()

        return carry

    lax.fori_loop(0, 3 * n + 10, tick, 0)
    for i in range(2):
        for s in range(4):
            ring_meta(i, s, s).wait_send()

    def ended(k, carry):
        for i in range(2):
            for s in range(4):
                back_ring(i, k, s).wait_send()
        return carry

    lax.fori_loop(0, n, ended, 0)
    for j in range(3 * n - 4, 3 * n):
        for what in range(4):
            x_copy(j, what).wait_send()
    for m in range(3):
        for what in range(8):
            w_copy(m, what).wait_send()
        sib_copy(m, 3).wait_send()
        y_copy(m, 2).wait_send()
        y_copy(m, 3).wait_send()


def shards(tokens, cotangent, expert_ids, gate_values, saved_pre, w_gate, w_up, w_down):
    width = tokens.shape[1]
    hidden = w_gate.shape[2]
    n = width // CH
    dma = pltpu.SemaphoreType.DMA
    vmem = pl.BlockSpec(memory_space=pltpu.VMEM)
    meta = jnp.concatenate(
        [
            jnp.pad(expert_ids.astype(F32).T, ((0, 2), (0, 0)), constant_values=-1.0),
            jnp.pad(gate_values.T, ((0, 2), (0, 0))),
        ],
        axis=0,
    )
    pre = saved_pre.reshape(NZ, NX, CAP, 2 * hidden)
    out, grad_gate, grad_up, grad_down = pl.pallas_call(
        kernel,
        out_shape=(
            jax.ShapeDtypeStruct((BLK, width), BF),
            jax.ShapeDtypeStruct((CH, hidden), BF),
            jax.ShapeDtypeStruct((CH, hidden), BF),
            jax.ShapeDtypeStruct((hidden, CH), BF),
        ),
        in_specs=[vmem] * 3 + [pl.BlockSpec(memory_space=pl.ANY)] + [vmem] * 3,
        out_specs=(vmem,) * 4,
        scratch_shapes=[
            pltpu.VMEM((NZ, 16, BLK), F32),
            pltpu.VMEM((n, NZ * BLK, CH), BF),
            pltpu.VMEM((2 * n, SLOTS, CH), BF),
            pltpu.VMEM((4, SLOTS, CH), BF),
            pltpu.VMEM((n, GRP, CH), BF),
            pltpu.VMEM((SLOTS, NZ * BLK), BF),
            pltpu.VMEM((SLOTS, 1), F32),
            pltpu.VMEM((KEEP, NZ * BLK, CH), F32),
            pltpu.VMEM((2, n, 4, BLK, CH), BF),
            pltpu.VMEM((3, n, CH, hidden), BF),
            pltpu.VMEM((SLOTS, hidden), F32),
            pltpu.VMEM((SLOTS, hidden), BF),
            pltpu.VMEM((SLOTS, hidden), BF),
            pltpu.VMEM((SLOTS, hidden), BF),
            pltpu.VMEM((2, NZ, CAP, 2 * hidden), BF),
            pltpu.VMEM((GRP, 2 * hidden), F32),
            pltpu.VMEM((CH, hidden), F32),
            pltpu.VMEM((3, CH, hidden), BF),
            pltpu.VMEM((3, NY, CH, hidden), BF),
            pltpu.VMEM((3, 2, CH, hidden), BF),
            pltpu.VMEM((3, CH, hidden), BF),
            pltpu.VMEM((3, 2, CH, hidden), BF),
            dma((2, 2 * n, 4)),
            dma((2, 2 * n, 4)),
            dma((2, 4)),
            dma((2, 4)),
            dma((3 * n, 6)),
            dma((3 * n, 6)),
            dma((2, n, 4)),
            dma((2, n, 4)),
            dma((3, 8)),
            dma((3, 8)),
            dma((3, NY)),
            dma((3, NY)),
            dma((3, 4)),
            dma((3, 4)),
            dma((NX,)),
        ],
        compiler_params=pltpu.CompilerParams(
            collective_id=0, has_side_effects=True, vmem_limit_bytes=62 * 2**20
        ),
        cost_estimate=pl.CostEstimate(flops=26 * 10**9, bytes_accessed=10 * 2**20, transcendentals=10**6),
        name="expert_backward",
    )(cotangent, tokens, meta, pre, w_gate[0], w_up[0], w_down[0])
    return (out, grad_gate[None], grad_up[None], grad_down[None])


def solution(mesh):
    tok = P(("dp", "expert"), None)
    row = P("expert", "dp", None)
    col = P("expert", None, "dp")
    return jax.shard_map(
        shards,
        mesh=mesh,
        in_specs=(tok, tok, tok, tok, P("expert", "dp", None, None, None), row, row, col),
        out_specs=(tok, row, row, col),
        check_vma=False,
    )
```

time: 422 us -> 221 us (0.52)
  waiting for transfers between devices: 244 us -> 0 us
  Pallas kernels: 0 us -> 203 us
  local copies, waits for them, and re-layouts: 80.2 us -> 15.2 us
  matrix products: 32.2 us -> 0 us
  starting transfers between devices: 24.9 us -> 0 us
  other arithmetic: 23.1 us -> 1.98 us
  between operations: 14.1 us -> 0.64 us
    all_to_all x3 -> x0, waiting for transfers between devices: 242 us -> none  [the longest x1 93.9 us: shards(): lax.all_to_all(slot_back, 'expert', split_axis=0, concat_axis=0, tiled=True)]
    pallas_call x0 -> x1, Pallas kernels: none -> 203 us  [shards(): pl.pallas_call(kernel, out_shape=(jax.ShapeDtypeStruct((BLK, width), BF),...]
    dot_general x6 -> x0, matrix products: 32.2 us -> none  [the longest x1 7.75 us: shards(): lax.dot_general(grad_gate_pre, gate_full, row_contract, preferred_element...]
    all_to_all x3 -> x0, starting transfers between devices: 24.6 us -> none  [the longest x1 11.8 us: shards(): lax.all_to_all(send_grads, 'expert', split_axis=0, concat_axis=0, tiled=T...]
    reshape x6 -> x0, local copies, waits for them, and re-layouts: 20.8 us -> none  [the longest x1 6.31 us: shards(): flat_back[target].reshape(tok_count, top_k, feat_width).astype(jnp.float32)]
    gather x4 -> x0, local copies, waits for them, and re-layouts: 19 us -> none  [the longest x2 9.77 us: shards(): tokens[slot_token]]
    convert_element_type x3 -> x0, local copies, waits for them, and re-layouts: 14.6 us -> none  [the longest x2 8.76 us: shards(): pre_act = saved_pre.reshape(-1, 2 * hidden).astype(jnp.float32)]
    scatter x3 -> x0, local copies, waits for them, and re-layouts: 10.1 us -> none  [the longest x1 3.38 us: shards(): jnp.zeros((experts * capacity,), jnp.int32).at[target].set(source_row)]
  transfers between devices with their start and end apart: 7 -> 0, of which waited for: 3 -> 0; matrix products, arithmetic and copies ran while one was open for 25% -> 0% of each run, Pallas kernels for 0% -> 0%
where the time goes in v2:
time: 221 us
  Pallas kernels  203 us (92%)
  local copies, waits for them, and re-layouts  15.2 us (7%)
    pallas_call x1, Pallas kernels, shards(): pl.pallas_call(kernel, out_shape=(jax.ShapeDtypeStruct((BLK, width), BF),...  203 us
    unnamed x7, local copies, waits for them, and re-layouts  15.2 us

profile of v2, /device:TPU:2, one launch (start us, length us, event | category | flops | bytes accessed | tf_op | source)
XLA Modules:
  0.0 220.6 jit_solution(9999870002951500671)
XLA Ops:
  0.6 0.7 convert_bitcast_fusion
  1.3 1.3 select_maximum_fusion.own_meta
  2.6 1.9 copy.13
  4.5 1.9 copy.14
  6.4 4.0 %copy.12 = bf16[1,1,32,26,1408]{4,3,2,1,0:T(8,128)(2,1)} copy(bf16[1,1,32,26,1408]{4,2,3,1,0:T(8,128)(2,1)} %param.12) | data formatting | bytes 4685824 | tf_op args[4]
  10.4 202.7 %expert_backward.1 = (bf16[128,2048]{1,0:T(8,128)(2,1)}, bf16[256,704]{1,0:T(8,128)(2,1)}, bf16[256,704]{1,0:T(8,128)(2,1)}, bf16[704,256]{1,0:T(8,128)(2,1)}) custom-call(bf16[128,2048]{1,0:T(8,128)(2,1)} %cot.1, bf16[128,2048]{1,0:T(8,128)(2,1)} %tok.1, f32[16,128]{1,0:T(8,128)} %select_maximum_fusion.own_meta, bf16[8,4,26,1408]{3,2,1,0:T(8,128)(2,1)} %bitcast.10, ...), custom_call_target="tpu_custom_call" | custom-call | flops 25999998976 | bytes 10485760 | tf_op jit(solution)/shard_map/expert_backward/pallas_call | solution.py:515
  213.2 1.9 copy.15
  215.1 1.9 copy.16
  217.0 1.9 copy.19
  218.8 1.7 copy.20

commit v3 on v2

v3 whole, which is shorter than its diff:
```python
import jax
import jax.numpy as jnp
from jax import lax
from jax.experimental import pallas as pl
from jax.experimental.pallas import tpu as pltpu
from jax.sharding import PartitionSpec as P

MESH = pl.DeviceIdType.MESH
NZ, NX, NY = 8, 4, 4
CAP = 26
TOP = 6
BLK = 128
GRP = NZ * CAP
SLOTS = NX * GRP
CH = 256
VIA = 112
KEEP = 5
HALF = BLK // 2
BF = jnp.bfloat16
F32 = jnp.float32


def nt(a, b):
    return lax.dot_general(a, b, (((1,), (1,)), ((), ())), preferred_element_type=F32)


def tn(a, b):
    return lax.dot_general(a, b, (((0,), (0,)), ((), ())), preferred_element_type=F32)


def nn(a, b):
    return jnp.dot(a, b, preferred_element_type=F32)


def span(start, size, unit):
    return pl.ds(pl.multiple_of(start, unit), size)


def build_picker(z, meta, pick, slot_gate):
    ids = meta[:, 0:8, :]
    gates = meta[:, 8:16, :]
    upper = (
        lax.broadcasted_iota(jnp.int32, (BLK, BLK), 0) < lax.broadcasted_iota(jnp.int32, (BLK, BLK), 1)
    ).astype(BF)
    row = lax.broadcasted_iota(jnp.int32, (GRP, BLK), 0)
    base = lax.broadcasted_iota(jnp.int32, (NZ, BLK), 0)
    for xp in range(NX):
        same = ids == (z * NX + xp).astype(F32)
        named = jnp.sum(jnp.where(same, 1.0, 0.0), axis=1)
        gate = jnp.sum(jnp.where(same, gates, 0.0), axis=1)
        earlier = nn(named.astype(BF), upper).astype(jnp.int32)
        key = jnp.where(named > 0.5, base + earlier * NZ, -1)
        total = jnp.zeros((GRP, BLK), F32)
        for zz in range(NZ):
            hit = row == key[zz : zz + 1, :]
            pick[xp * GRP : (xp + 1) * GRP, zz * BLK : (zz + 1) * BLK] = jnp.where(hit, 1.0, 0.0).astype(BF)
            total = total + jnp.where(hit, gate[zz : zz + 1, :], 0.0)
        slot_gate[xp * GRP : (xp + 1) * GRP, :] = jnp.sum(total, axis=1, keepdims=True)


def kernel(
    cot, tok, ids, gates, pre, w_gate, w_up, w_down, out, grads,
    meta, ag, slot, stage, relay, pick, pick_t, slot_gate, part, z_in, weights, g_gate, g_up, hid, act_t,
    pre_in, pre32, tmp, rows32, sib_out, sib_in, y_out, y_half, y_full,
    z_send, z_recv, m_send, m_recv, x_send, x_recv, b_send, b_recv, w_send, w_recv, s_send, s_recv, y_send, y_recv, p_sem,
):
    r, e = lax.axis_index("dp"), lax.axis_index("expert")
    y, c = r // 2, lax.rem(r, 2)
    z, x = e // NX, lax.rem(e, NX)
    hidden = w_gate.shape[0]
    half_hid = hidden // 2
    n = cot.shape[1] // CH

    def at(yy=y, cc=c, zz=z, xx=x):
        return (yy * 2 + cc, zz * NX + xx)

    z_to = (at(zz=lax.rem(z + 1, NZ)), at(zz=lax.rem(z + NZ - 1, NZ)))
    x_to = (at(xx=lax.rem(x + 1, NX)), at(xx=lax.rem(x + NX - 1, NX)))
    y_to = (at(yy=lax.rem(y + 1, NY)), at(yy=lax.rem(y + NY - 1, NY)))
    sibling = at(cc=1 - c)
    z_step = (1, NZ - 1)
    low = lax.rem(y + NY - 1, NY)
    high = lax.rem(y + 1, NY)
    far_y = lax.rem(y + 2, NY)
    own = y * 2 + c
    upper_half, lower_half = slice(0, half_hid), slice(half_hid, hidden)
    barrier = pltpu.get_barrier_semaphore()
    peers = (*z_to, *x_to, *y_to, sibling)
    for peer in peers:
        pl.semaphore_signal(barrier, inc=1, device_id=peer, device_id_type=MESH)
    pl.semaphore_wait(barrier, len(peers))

    def send(src, dst, s_sem, r_sem, to):
        return pltpu.make_async_remote_copy(
            src_ref=src, dst_ref=dst, send_sem=s_sem, recv_sem=r_sem, device_id=to, device_id_type=MESH
        )

    def block_of(k):
        q = k // 2
        off = 2 - q + 3 * (q // 2) - 2 * (q // 3)
        core = c + (1 - 2 * c) * (1 - lax.rem(k, 2))
        return lax.rem(y + off, NY) * 2 + core

    def w_copy(m, what):
        view, to = (
            (weights.at[m, own], y_to[0]),
            (weights.at[m, own], y_to[1]),
            (weights.at[m, low * 2 + c, upper_half, :], y_to[0]),
            (weights.at[m, high * 2 + c, lower_half, :], y_to[1]),
            (weights.at[m, own], sibling),
            (weights.at[m, low * 2 + c], sibling),
            (weights.at[m, high * 2 + c], sibling),
            (weights.at[m, far_y * 2 + c], sibling),
        )[what]
        return send(view, view, w_send.at[m, what], w_recv.at[m, what], to)

    def w_arrival(m, what):
        view, source = (
            (weights.at[m, low * 2 + c], y_to[1]),
            (weights.at[m, high * 2 + c], y_to[0]),
            (weights.at[m, far_y * 2 + c, upper_half, :], y_to[1]),
            (weights.at[m, far_y * 2 + c, lower_half, :], y_to[0]),
            (weights.at[m, y * 2 + 1 - c], sibling),
            (weights.at[m, low * 2 + 1 - c], sibling),
            (weights.at[m, high * 2 + 1 - c], sibling),
            (weights.at[m, far_y * 2 + 1 - c], sibling),
        )[what]
        return send(view, view, w_send.at[m, what], w_recv.at[m, what], source)

    def w_start(m):
        for what in (0, 1, 4):
            w_copy(m, what).start()

    def w_forward(m):
        for i in range(2):
            w_arrival(m, i).wait_recv()
            w_copy(m, 2 + i).start()
            w_copy(m, 5 + i).start()

    def w_far(m):
        for i in range(2):
            w_arrival(m, 2 + i).wait_recv()
        w_copy(m, 7).start()

    def w_done(m):
        for what in range(4, 8):
            w_arrival(m, what).wait_recv()

    def ring(i, j, s, p, dist):
        origin = lax.rem(z + dist * (NZ - z_step[i]), NZ)
        jn = lax.rem(j, n)
        view = ag.at[jn, span(origin * BLK + p * HALF, HALF, HALF), :]
        return send(view, view, z_send.at[i, jn, s, p], z_recv.at[i, jn, s, p], z_to[i])

    def ring_meta(i, s, dist):
        origin = lax.rem(z + dist * (NZ - z_step[i]), NZ)
        view = meta.at[origin, i * 8 : i * 8 + 8, :] if s == 3 else meta.at[origin]
        return send(view, view, m_send.at[i, s], m_recv.at[i, s], z_to[i])

    def x_copy(j, what):
        i = what % 2
        st, sl, rl = lax.rem(j, 4), lax.rem(j, 2 * n), lax.rem(j, n)
        near = lax.rem(x + (1 if i == 0 else NX - 1), NX) * GRP
        far = lax.rem(x + 2, NX) * GRP
        other = lax.rem(x + (NX - 1 if i == 0 else 1), NX) * GRP
        lo, size = (0, VIA) if i == 0 else (VIA, GRP - VIA)
        if what < 2:
            src, dst = stage.at[st, span(near, GRP, 16), :], slot.at[sl, span(x * GRP, GRP, 16), :]
        elif what < 4:
            src, dst = stage.at[st, span(far + lo, size, 16), :], relay.at[rl, lo : lo + size, :]
        else:
            src, dst = relay.at[rl, lo : lo + size, :], slot.at[sl, span(other + lo, size, 16), :]
        return send(src, dst, x_send.at[rl, what], x_recv.at[rl, what], x_to[i])

    def x_arrival(j, what):
        i = what % 2
        sl, rl = lax.rem(j, 2 * n), lax.rem(j, n)
        other = lax.rem(x + (NX - 1 if i == 0 else 1), NX) * GRP
        far = lax.rem(x + 2, NX) * GRP
        lo, size = (0, VIA) if i == 0 else (VIA, GRP - VIA)
        if what < 2:
            view = slot.at[sl, span(other, GRP, 16), :]
        elif what < 4:
            view = relay.at[rl, lo : lo + size, :]
        else:
            view = slot.at[sl, span(far + lo, size, 16), :]
        return send(view, view, x_send.at[rl, what], x_recv.at[rl, what], x_to[1 - i])

    def back_out(i, k, s, p):
        first = (i * 4 + s) * BLK + p * HALF
        return ag.at[k, first : first + HALF, :]

    def back_ring(i, k, s, p):
        dst = z_in.at[i, k, s, p * HALF : (p + 1) * HALF, :]
        return send(back_out(i, k, s, p), dst, b_send.at[i, k, s, p], b_recv.at[i, k, s, p], z_to[i])

    def sib_copy(m, q):
        return send(sib_out.at[m], sib_in.at[m, q], s_send.at[m, q], s_recv.at[m, q], sibling)

    def y_copy(m, what):
        src, dst, to = (
            (y_out.at[m, 0, upper_half, :], y_half.at[m, upper_half, :], y_to[0]),
            (y_out.at[m, 0, lower_half, :], y_half.at[m, lower_half, :], y_to[1]),
            (y_out.at[m, 1], y_full.at[m, 0], y_to[0]),
            (y_out.at[m, 0], y_full.at[m, 1], y_to[1]),
        )[what]
        return send(src, dst, y_send.at[m, what], y_recv.at[m, what], to)

    def reduce_block(m, k, chunk):
        q = k // 2
        tmp[...] = nn(act_t[m], slot[chunk])

        @pl.when(lax.rem(k, 2) == 0)
        def _():
            @pl.when(q > 0)
            def _():
                sib_copy(m, q - 1).wait_send()

            sib_out[m] = tmp[...].astype(BF)
            sib_copy(m, q).start()

        @pl.when(lax.rem(k, 2) == 1)
        def _():
            sib_copy(m, q).wait_recv()
            tmp[...] += sib_in[m, q].astype(F32)

        @pl.when(k == 1)
        def _():
            y_out[m, 0] = tmp[...].astype(BF)
            y_copy(m, 0).start()
            y_copy(m, 1).start()

        @pl.when(k == 3)
        def _():
            y_copy(m, 0).wait_recv()
            tmp[upper_half, :] += y_half[m, upper_half, :].astype(F32)
            y_out[m, 1] = tmp[...].astype(BF)
            y_copy(m, 2).start()

        @pl.when(k == 5)
        def _():
            y_copy(m, 0).wait_send()
            y_copy(m, 1).wait_send()
            y_copy(m, 1).wait_recv()
            tmp[lower_half, :] += y_half[m, lower_half, :].astype(F32)
            y_out[m, 0] = tmp[...].astype(BF)
            y_copy(m, 3).start()

        @pl.when(k == 7)
        def _():
            y_copy(m, 2).wait_recv()
            y_copy(m, 3).wait_recv()
            grads[m] = (tmp[...] + y_full[m, 0].astype(F32) + y_full[m, 1].astype(F32)).astype(BF)

    depth = 16 * NX
    steps = SLOTS // depth

    def pre_copy(b):
        buf = lax.rem(b, 4)
        return pltpu.make_async_copy(pre.at[span(b * depth, depth, depth), :], pre_in.at[buf], p_sem.at[buf])

    def activations(b):
        pre_copy(b).wait()
        row = lax.broadcasted_iota(jnp.int32, (depth, depth), 0)
        column = lax.broadcasted_iota(jnp.int32, (depth, depth), 1)
        order = jnp.where(column == lax.rem(row, 16) * NX + row // 16, 1.0, 0.0).astype(BF)
        pre32[...] = nn(order, pre_in[lax.rem(b, 4)])

        @pl.when(b + 4 < steps)
        def _():
            pre_copy(b + 4).start()

        for xx in range(NX):
            src = slice(xx * 16, (xx + 1) * 16)
            gate, up = pre32[src, :hidden], pre32[src, hidden:]
            sig = 1.0 / (1.0 + jnp.exp(-gate))
            dst = span(xx * GRP + b * 16, 16, 16)
            g_gate[dst, :] = (up * sig * (1.0 + gate * (1.0 - sig))).astype(BF)
            g_up[dst, :] = (gate * sig).astype(BF)
            hid[dst, :] = (gate * sig * up).astype(BF)

    for b in range(4):
        pre_copy(b).start()
    mine = span(z * BLK, BLK, BLK)
    meta[z] = jnp.full(meta.shape[1:], -1.0, F32)
    meta[z, 0:TOP, :] = ids[...].astype(F32)
    meta[z, 8 : 8 + TOP, :] = gates[...]
    weights[0, own] = w_down[...]
    w_start(0)
    weights[1, own] = w_gate[...]
    weights[2, own] = w_up[...]
    tiles = [slice(b, min(b + CH, hidden)) for b in range(0, hidden, CH)]
    for b in range(len(tiles)):
        part[b, 0:SLOTS, :] = jnp.zeros((SLOTS, CH), F32)

    def sub_tick(t, p):
        for s in (4, 3, 2, 1, 0):
            j = t - s

            @pl.when((j >= 0) & (j < 2 * n))
            def _():
                if s > 0:
                    if p == 0:

                        @pl.when(j == 0)
                        def _():
                            for i in range(2):
                                ring_meta(i, s - 1, s).wait_recv()
                                if s < 4:
                                    ring_meta(i, s, s).start()

                    for i in range(2):
                        last = 3 if p == i else 2
                        if s - 1 <= last:
                            ring(i, j, s - 1, p, s).wait_recv()
                        if s <= last:
                            ring(i, j, s, p, s).start()
                else:
                    if p == 0:

                        @pl.when(j == 0)
                        def _():
                            for i in range(2):
                                ring_meta(i, 0, 0).start()

                        columns = span(block_of(lax.rem(j, n)) * CH, CH, CH)

                        @pl.when(j < n)
                        def _():
                            ag[lax.rem(j, n), mine, :] = cot[:, columns]

                        @pl.when(j >= n)
                        def _():
                            ag[lax.rem(j, n), mine, :] = tok[:, columns]

                    for i in range(2):
                        ring(i, j, 0, p, 0).start()

        for s in (4, 3, 2, 1):
            k = t - (2 * n + 6) - s
            kp = lax.rem(k + KEEP, KEEP)
            half = slice(p * HALF, (p + 1) * HALF)

            @pl.when((k >= 0) & (k < n))
            def _():
                if s == 4:
                    total = part[kp, span(z * BLK + p * HALF, HALF, HALF), :]
                    for i in range(2):
                        back_ring(i, k, 3, p).wait_recv()
                        total = total + z_in[i, k, 3, half, :].astype(F32)
                    out[half, span(block_of(k) * CH, CH, CH)] = total.astype(BF)
                else:
                    for i in range(2):
                        dest = lax.rem(z + z_step[i] * (4 - s), NZ)
                        value = part[kp, span(dest * BLK + p * HALF, HALF, HALF), :]
                        if s > 1 or p == i:
                            back_ring(i, k, s - 1, p).wait_recv()
                            value = value + z_in[i, k, s - 1, half, :].astype(F32)
                        back_out(i, k, s, p)[...] = value.astype(BF)
                        back_ring(i, k, s, p).start()

    def tick(t, carry):
        sub_tick(t, 0)

        ja = t - 6

        @pl.when((ja >= 0) & (ja < 3 * n))
        def _():
            for what in (0, 1, 4, 5):
                x_arrival(ja, what).wait_recv()

        @pl.when((ja >= 1) & (ja < 3 * n + 1))
        def _():
            for what in (4, 5):
                x_copy(ja - 1, what).wait_send()

        for when, step in (
            (3, lambda: (w_forward(0), w_start(1))),
            (5, lambda: w_far(0)),
            (6, lambda: (w_done(0), w_forward(1), w_start(2))),
            (8, lambda: w_far(1)),
            (9, lambda: w_forward(2)),
            (10, lambda: w_done(1)),
            (11, lambda: w_far(2)),
            (13, lambda: w_done(2)),
        ):

            @pl.when(t == when)
            def _():
                step()

        @pl.when(t < 4)
        def _():
            def some(q, carry):
                @pl.when(t * 4 + q < steps)
                def _():
                    activations(t * 4 + q)

                return carry

            lax.fori_loop(0, 4, some, 0)

        @pl.when(t == 4)
        def _():
            act_t[0] = hid[...].T

        @pl.when((t >= 5) & (t < 5 + NZ))
        def _():
            block = span((t - 5) * BLK, BLK, BLK)
            pick_t[block, :] = pick[:, block].T

        @pl.when((ja >= 0) & (ja < n))
        def _():
            block = block_of(ja)
            for b, cols in enumerate(tiles):
                part[b, 0:SLOTS, 0 : cols.stop - cols.start] += nt(slot[ja], weights[0, block, cols, :])

        @pl.when(ja == n - 1)
        def _():
            for b, cols in enumerate(tiles):
                grad = part[b, 0:SLOTS, 0 : cols.stop - cols.start]
                g_gate[:, cols] = (grad * g_gate[:, cols].astype(F32)).astype(BF)
                g_up[:, cols] = (grad * g_up[:, cols].astype(F32)).astype(BF)
            act_t[1] = g_gate[...].T
            act_t[2] = g_up[...].T

        @pl.when((ja >= 3) & (ja < n + 3))
        def _():
            reduce_block(0, ja - 3, ja - 3)

        @pl.when((ja >= n) & (ja < 2 * n))
        def _():
            reduce_block(1, ja - n, ja)
            reduce_block(2, ja - n, ja)

        @pl.when((ja >= 2 * n) & (ja < 3 * n))
        def _():
            k = ja - 2 * n
            kp = lax.rem(k, KEEP)
            part[kp] = nn(pick_t[...], slot[k])
            dest = lax.rem(z + 4, NZ)
            for i in range(2):
                value = part[kp, span(dest * BLK + i * HALF, HALF, HALF), :]
                back_out(i, k, 0, i)[...] = value.astype(BF)
                back_ring(i, k, 0, i).start()

        jr = t - 5

        @pl.when((jr >= 0) & (jr < 3 * n))
        def _():
            for i in range(2):
                x_arrival(jr, 2 + i).wait_recv()
                x_copy(jr, 4 + i).start()

        @pl.when((jr >= 0) & (jr < 2 * n))
        def _():
            for i in range(2):
                for p in range(2):
                    for s in range(4 if p == i else 3):
                        ring(i, jr, s, p, s).wait_send()

        sub_tick(t, 1)

        j = t - 4

        @pl.when(j == 0)
        def _():
            build_picker(z, meta, pick, slot_gate)

        @pl.when((j >= 4) & (j < 3 * n))
        def _():
            for what in range(4):
                x_copy(j - 4, what).wait_send()

        @pl.when((j >= 0) & (j < 2 * n))
        def _():
            plain = (j >= n).astype(F32)
            rows32[...] = nn(pick[...], ag[lax.rem(j, n)]) * (slot_gate[...] * (1.0 - plain) + plain)

        @pl.when((j >= 2 * n) & (j < 3 * n))
        def _():
            block = block_of(j - 2 * n)
            rows32[...] = nn(g_gate[...], weights[1, block]) + nn(g_up[...], weights[2, block])

        @pl.when((j >= 0) & (j < 3 * n))
        def _():
            for d in (2, 1, 3, 0):
                rows = span(lax.rem(x + d, NX) * GRP, GRP, 16)
                if d == 0:
                    slot[lax.rem(j, 2 * n), rows, :] = rows32[rows, :].astype(BF)
                else:
                    stage[lax.rem(j, 4), rows, :] = rows32[rows, :].astype(BF)
                for what in {2: (2, 3), 1: (0,), 3: (1,), 0: ()}[d]:
                    x_copy(j, what).start()

        return carry

    lax.fori_loop(0, 3 * n + 10, tick, 0)
    for i in range(2):
        for s in range(4):
            ring_meta(i, s, s).wait_send()

    def ended(k, carry):
        for i in range(2):
            for p in range(2):
                for s in range(0 if p == i else 1, 4):
                    back_ring(i, k, s, p).wait_send()
        return carry

    lax.fori_loop(0, n, ended, 0)
    for j in range(3 * n - 4, 3 * n):
        for what in range(4):
            x_copy(j, what).wait_send()
    for m in range(3):
        for what in range(8):
            w_copy(m, what).wait_send()
        sib_copy(m, 3).wait_send()
        y_copy(m, 2).wait_send()
        y_copy(m, 3).wait_send()


def hand_out(rows, grads, out, grad_gate, grad_up, grad_down, sem):
    copies = [pltpu.make_async_copy(rows, out, sem.at[0])]
    for m, to in ((1, grad_gate), (2, grad_up), (0, grad_down)):
        copies.append(pltpu.make_async_copy(grads.at[m], to, sem.at[1 + m]))
    for copy in copies:
        copy.start()
    for copy in copies:
        copy.wait()


def shards(tokens, cotangent, expert_ids, gate_values, saved_pre, w_gate, w_up, w_down):
    width = tokens.shape[1]
    hidden = w_gate.shape[2]
    n = width // CH
    dma = pltpu.SemaphoreType.DMA
    vmem = pl.BlockSpec(memory_space=pltpu.VMEM)
    hbm = pl.BlockSpec(memory_space=pl.ANY)
    pre = saved_pre.reshape(NZ * NX, CAP, 2 * hidden).transpose(1, 0, 2).reshape(SLOTS, 2 * hidden)
    shape = jax.ShapeDtypeStruct
    rows, grads = pl.pallas_call(
        kernel,
        out_shape=(shape((BLK, width), BF), shape((3, hidden, CH), BF)),
        in_specs=[vmem] * 4 + [hbm] + [vmem] * 3,
        out_specs=(vmem, vmem),
        scratch_shapes=[
            pltpu.VMEM((NZ, 16, BLK), F32),
            pltpu.VMEM((n, NZ * BLK, CH), BF),
            pltpu.VMEM((2 * n, SLOTS, CH), BF),
            pltpu.VMEM((4, SLOTS, CH), BF),
            pltpu.VMEM((n, GRP, CH), BF),
            pltpu.VMEM((SLOTS, NZ * BLK), BF),
            pltpu.VMEM((NZ * BLK, SLOTS), BF),
            pltpu.VMEM((SLOTS, 1), F32),
            pltpu.VMEM((KEEP, NZ * BLK, CH), F32),
            pltpu.VMEM((2, n, 4, BLK, CH), BF),
            pltpu.VMEM((3, n, hidden, CH), BF),
            pltpu.VMEM((SLOTS, hidden), BF),
            pltpu.VMEM((SLOTS, hidden), BF),
            pltpu.VMEM((SLOTS, hidden), BF),
            pltpu.VMEM((3, hidden, SLOTS), BF),
            pltpu.VMEM((4, 16 * NX, 2 * hidden), BF),
            pltpu.VMEM((16 * NX, 2 * hidden), F32),
            pltpu.VMEM((hidden, CH), F32),
            pltpu.VMEM((SLOTS, CH), F32),
            pltpu.VMEM((3, hidden, CH), BF),
            pltpu.VMEM((3, NY, hidden, CH), BF),
            pltpu.VMEM((3, 2, hidden, CH), BF),
            pltpu.VMEM((3, hidden, CH), BF),
            pltpu.VMEM((3, 2, hidden, CH), BF),
            dma((2, n, 4, 2)),
            dma((2, n, 4, 2)),
            dma((2, 4)),
            dma((2, 4)),
            dma((n, 6)),
            dma((n, 6)),
            dma((2, n, 4, 2)),
            dma((2, n, 4, 2)),
            dma((3, 8)),
            dma((3, 8)),
            dma((3, NY)),
            dma((3, NY)),
            dma((3, 4)),
            dma((3, 4)),
            dma((4,)),
        ],
        compiler_params=pltpu.CompilerParams(
            collective_id=0, has_side_effects=True, vmem_limit_bytes=62 * 2**20
        ),
        cost_estimate=pl.CostEstimate(flops=26 * 10**9, bytes_accessed=10 * 2**20, transcendentals=10**6),
        name="expert_backward",
    )(cotangent, tokens, expert_ids.T, gate_values.T, pre, w_gate[0].T, w_up[0].T, w_down[0])
    out, grad_gate, grad_up, grad_down = pl.pallas_call(
        hand_out,
        out_shape=(shape((BLK, width), BF), *[shape((hidden, CH), BF)] * 3),
        in_specs=[hbm] * 2,
        out_specs=(hbm,) * 4,
        scratch_shapes=[dma((4,))],
        name="hand_out",
    )(rows, grads)
    return (out, grad_gate.T[None], grad_up.T[None], grad_down[None])


def solution(mesh):
    tok = P(("dp", "expert"), None)
    row = P("expert", "dp", None)
    col = P("expert", None, "dp")
    return jax.shard_map(
        shards,
        mesh=mesh,
        in_specs=(tok, tok, tok, tok, P("expert", "dp", None, None, None), row, row, col),
        out_specs=(tok, row, row, col),
        check_vma=False,
    )
```

time: 221 us -> 240 us (1.086)
  Pallas kernels: 203 us -> 240 us
  local copies, waits for them, and re-layouts: 15.2 us -> 0 us
    pallas_call x1 -> x2, Pallas kernels: 203 us -> 240 us  [the longest x1 190 us: shards(): pl.pallas_call(kernel, out_shape=(shape((BLK, width), BF), shape((3, hidd...]
    unnamed x7 -> x0, local copies, waits for them, and re-layouts: 15.2 us -> none
where the time goes in v3:
time: 240 us
  Pallas kernels  240 us (100%)
    pallas_call x1, Pallas kernels, shards(): pl.pallas_call(kernel, out_shape=(shape((BLK, width), BF), shape((3, hidd...  190 us
    pallas_call x1, Pallas kernels, shards(): pl.pallas_call(hand_out, out_shape=(shape((BLK, width), BF), *[shape((hid...  49.8 us

profile of v3, /device:TPU:2, one launch (start us, length us, event | category | flops | bytes accessed | tf_op | source)
XLA Modules:
  0.0 240.3 jit_solution(8380391492189364081)
XLA Ops:
  0.6 189.9 %expert_backward.1 = (bf16[128,2048]{1,0:T(8,128)(2,1)}, bf16[3,704,256]{2,1,0:T(8,128)(2,1)}) custom-call(bf16[128,2048]{1,0:T(8,128)(2,1)} %cot.1, bf16[128,2048]{1,0:T(8,128)(2,1)} %tok.1, s32[6,128]{1,0:T(8,128)} %bitcast.28, f32[6,128]{1,0:T(8,128)} %bitcast.29, bf16[832,1408]{1,0:T(8,128)(2,1)} %bitcast.21, bf16[704,256]{1,0:T(8,128)(2,1)} %bitcast.22, ...), custom_call_target="tpu_custom_call" | custom-call | flops 25999998976 | bytes 10485760 | tf_op jit(solution)/shard_map/expert_backward/pallas_call | solution.py:541
  190.5 49.8 %hand_out.1 = (bf16[128,2048]{1,0:T(8,128)(2,1)}, bf16[704,256]{1,0:T(8,128)(2,1)}, bf16[704,256]{1,0:T(8,128)(2,1)}, bf16[704,256]{1,0:T(8,128)(2,1)}) custom-call(bf16[128,2048]{1,0:T(8,128)(2,1)} %get-tuple-element.10.rows, bf16[3,704,256]{2,1,0:T(8,128)(2,1)} %get-tuple-element.11.grads), custom_call_target="tpu_custom_call" | custom-call | tf_op jit(solution)/shard_map/hand_out/pallas_call | solution.py:593

commit v4 on v3

--- a/solution.py
+++ b/solution.py
@@ -14,7 +14,10 @@
 SLOTS = NX * GRP
 CH = 256
 VIA = 112
-KEEP = 5
+LAG = 2
+X_LAG = 2
+SUM_LAG = 2
+AG_SLOTS = 12
 HALF = BLK // 2
 BF = jnp.bfloat16
 F32 = jnp.float32
@@ -60,7 +63,7 @@
 
 def kernel(
     cot, tok, ids, gates, pre, w_gate, w_up, w_down, out, grads,
-    meta, ag, slot, stage, relay, pick, pick_t, slot_gate, part, z_in, weights, g_gate, g_up, hid, act_t,
+    meta, ag, slot, stage, relay, pick, pick_t, slot_gate, part, z_in, weights, gh, g_gate, g_up, act_t,
     pre_in, pre32, tmp, rows32, sib_out, sib_in, y_out, y_half, y_full,
     z_send, z_recv, m_send, m_recv, x_send, x_recv, b_send, b_recv, w_send, w_recv, s_send, s_recv, y_send, y_recv, p_sem,
 ):
@@ -146,11 +149,11 @@
         for what in range(4, 8):
             w_arrival(m, what).wait_recv()
 
-    def ring(i, j, s, p, dist):
+    def ring(i, j, s, dist):
         origin = lax.rem(z + dist * (NZ - z_step[i]), NZ)
-        jn = lax.rem(j, n)
-        view = ag.at[jn, span(origin * BLK + p * HALF, HALF, HALF), :]
-        return send(view, view, z_send.at[i, jn, s, p], z_recv.at[i, jn, s, p], z_to[i])
+        rows = span(origin * BLK + i * HALF, HALF, HALF) if s == 3 else span(origin * BLK, BLK, BLK)
+        view = ag.at[lax.rem(j, AG_SLOTS), rows, :]
+        return send(view, view, z_send.at[i, j, s], z_recv.at[i, j, s], z_to[i])
 
     def ring_meta(i, s, dist):
         origin = lax.rem(z + dist * (NZ - z_step[i]), NZ)
@@ -186,13 +189,13 @@
             view = slot.at[sl, span(far + lo, size, 16), :]
         return send(view, view, x_send.at[rl, what], x_recv.at[rl, what], x_to[1 - i])
 
-    def back_out(i, k, s, p):
-        first = (i * 4 + s) * BLK + p * HALF
-        return ag.at[k, first : first + HALF, :]
-
-    def back_ring(i, k, s, p):
-        dst = z_in.at[i, k, s, p * HALF : (p + 1) * HALF, :]
-        return send(back_out(i, k, s, p), dst, b_send.at[i, k, s, p], b_recv.at[i, k, s, p], z_to[i])
+    def back_out(i, k, s):
+        first = (i * 4 + s) * BLK
+        return ag.at[AG_SLOTS - n + k, first : first + (HALF if s == 0 else BLK), :]
+
+    def back_ring(i, k, s):
+        dst = z_in.at[i, k, s, 0 : HALF if s == 0 else BLK, :]
+        return send(back_out(i, k, s), dst, b_send.at[i, k, s], b_recv.at[i, k, s], z_to[i])
 
     def sib_copy(m, q):
         return send(sib_out.at[m], sib_in.at[m, q], s_send.at[m, q], s_recv.at[m, q], sibling)
@@ -252,6 +255,8 @@
             y_copy(m, 3).wait_recv()
             grads[m] = (tmp[...] + y_full[m, 0].astype(F32) + y_full[m, 1].astype(F32)).astype(BF)
 
+    tiles = [slice(b, min(b + CH, hidden)) for b in range(0, hidden, CH)]
+
     depth = 16 * NX
     steps = SLOTS // depth
 
@@ -277,7 +282,9 @@
             dst = span(xx * GRP + b * 16, 16, 16)
             g_gate[dst, :] = (up * sig * (1.0 + gate * (1.0 - sig))).astype(BF)
             g_up[dst, :] = (gate * sig).astype(BF)
-            hid[dst, :] = (gate * sig * up).astype(BF)
+            act = (gate * sig * up).astype(BF)
+            for i, cols in enumerate(tiles):
+                stage[i, dst, 0 : cols.stop - cols.start] = act[:, cols]
 
     for b in range(4):
         pre_copy(b).start()
@@ -289,162 +296,77 @@
     w_start(0)
     weights[1, own] = w_gate[...]
     weights[2, own] = w_up[...]
-    tiles = [slice(b, min(b + CH, hidden)) for b in range(0, hidden, CH)]
     for b in range(len(tiles)):
-        part[b, 0:SLOTS, :] = jnp.zeros((SLOTS, CH), F32)
-
-    def sub_tick(t, p):
+        gh[b] = jnp.zeros((SLOTS, CH), F32)
+
+    gather_at = 4 * LAG
+    relay_at = gather_at + X_LAG
+    ready_at = gather_at + 2 * X_LAG
+    early = n // 2
+    back_at = n + early
+    late_at = back_at + n
+    sums_at = back_at + ready_at
+
+    def tick(t, carry):
         for s in (4, 3, 2, 1, 0):
-            j = t - s
+            j = t - LAG * s
 
             @pl.when((j >= 0) & (j < 2 * n))
             def _():
-                if s > 0:
-                    if p == 0:
-
-                        @pl.when(j == 0)
-                        def _():
-                            for i in range(2):
-                                ring_meta(i, s - 1, s).wait_recv()
-                                if s < 4:
-                                    ring_meta(i, s, s).start()
-
+                @pl.when(j == 0)
+                def _():
                     for i in range(2):
-                        last = 3 if p == i else 2
-                        if s - 1 <= last:
-                            ring(i, j, s - 1, p, s).wait_recv()
-                        if s <= last:
-                            ring(i, j, s, p, s).start()
-                else:
-                    if p == 0:
-
-                        @pl.when(j == 0)
-                        def _():
-                            for i in range(2):
-                                ring_meta(i, 0, 0).start()
-
-                        columns = span(block_of(lax.rem(j, n)) * CH, CH, CH)
-
-                        @pl.when(j < n)
-                        def _():
-                            ag[lax.rem(j, n), mine, :] = cot[:, columns]
-
-                        @pl.when(j >= n)
-                        def _():
-                            ag[lax.rem(j, n), mine, :] = tok[:, columns]
-
-                    for i in range(2):
-                        ring(i, j, 0, p, 0).start()
+                        if s > 0:
+                            ring_meta(i, s - 1, s).wait_recv()
+                        if s < 4:
+                            ring_meta(i, s, s).start()
+
+                if s == 0:
+                    columns = span(block_of(lax.rem(j, n)) * CH, CH, CH)
+
+                    @pl.when(j < n)
+                    def _():
+                        ag[lax.rem(j, AG_SLOTS), mine, :] = cot[:, columns]
+
+                    @pl.when(j >= n)
+                    def _():
+                        ag[lax.rem(j, AG_SLOTS), mine, :] = tok[:, columns]
+
+                for i in range(2):
+                    if s > 0:
+                        ring(i, j, s - 1, s).wait_recv()
+                    if s < 4:
+                        ring(i, j, s, s).start()
 
         for s in (4, 3, 2, 1):
-            k = t - (2 * n + 6) - s
-            kp = lax.rem(k + KEEP, KEEP)
-            half = slice(p * HALF, (p + 1) * HALF)
+            k = t - sums_at - SUM_LAG * s
 
             @pl.when((k >= 0) & (k < n))
             def _():
                 if s == 4:
-                    total = part[kp, span(z * BLK + p * HALF, HALF, HALF), :]
+                    total = part[k, mine, :].astype(F32)
                     for i in range(2):
-                        back_ring(i, k, 3, p).wait_recv()
-                        total = total + z_in[i, k, 3, half, :].astype(F32)
-                    out[half, span(block_of(k) * CH, CH, CH)] = total.astype(BF)
+                        back_ring(i, k, 3).wait_recv()
+                        total = total + z_in[i, k, 3].astype(F32)
+                    out[:, span(block_of(k) * CH, CH, CH)] = total.astype(BF)
                 else:
                     for i in range(2):
                         dest = lax.rem(z + z_step[i] * (4 - s), NZ)
-                        value = part[kp, span(dest * BLK + p * HALF, HALF, HALF), :]
-                        if s > 1 or p == i:
-                            back_ring(i, k, s - 1, p).wait_recv()
-                            value = value + z_in[i, k, s - 1, half, :].astype(F32)
-                        back_out(i, k, s, p)[...] = value.astype(BF)
-                        back_ring(i, k, s, p).start()
-
-    def tick(t, carry):
-        sub_tick(t, 0)
-
-        ja = t - 6
-
-        @pl.when((ja >= 0) & (ja < 3 * n))
-        def _():
-            for what in (0, 1, 4, 5):
-                x_arrival(ja, what).wait_recv()
-
-        @pl.when((ja >= 1) & (ja < 3 * n + 1))
-        def _():
-            for what in (4, 5):
-                x_copy(ja - 1, what).wait_send()
-
-        for when, step in (
-            (3, lambda: (w_forward(0), w_start(1))),
-            (5, lambda: w_far(0)),
-            (6, lambda: (w_done(0), w_forward(1), w_start(2))),
-            (8, lambda: w_far(1)),
-            (9, lambda: w_forward(2)),
-            (10, lambda: w_done(1)),
-            (11, lambda: w_far(2)),
-            (13, lambda: w_done(2)),
-        ):
-
-            @pl.when(t == when)
-            def _():
-                step()
-
-        @pl.when(t < 4)
-        def _():
-            def some(q, carry):
-                @pl.when(t * 4 + q < steps)
-                def _():
-                    activations(t * 4 + q)
-
-                return carry
-
-            lax.fori_loop(0, 4, some, 0)
-
-        @pl.when(t == 4)
-        def _():
-            act_t[0] = hid[...].T
-
-        @pl.when((t >= 5) & (t < 5 + NZ))
-        def _():
-            block = span((t - 5) * BLK, BLK, BLK)
-            pick_t[block, :] = pick[:, block].T
-
-        @pl.when((ja >= 0) & (ja < n))
-        def _():
-            block = block_of(ja)
-            for b, cols in enumerate(tiles):
-                part[b, 0:SLOTS, 0 : cols.stop - cols.start] += nt(slot[ja], weights[0, block, cols, :])
-
-        @pl.when(ja == n - 1)
-        def _():
-            for b, cols in enumerate(tiles):
-                grad = part[b, 0:SLOTS, 0 : cols.stop - cols.start]
-                g_gate[:, cols] = (grad * g_gate[:, cols].astype(F32)).astype(BF)
-                g_up[:, cols] = (grad * g_up[:, cols].astype(F32)).astype(BF)
-            act_t[1] = g_gate[...].T
-            act_t[2] = g_up[...].T
-
-        @pl.when((ja >= 3) & (ja < n + 3))
-        def _():
-            reduce_block(0, ja - 3, ja - 3)
-
-        @pl.when((ja >= n) & (ja < 2 * n))
-        def _():
-            reduce_block(1, ja - n, ja)
-            reduce_block(2, ja - n, ja)
-
-        @pl.when((ja >= 2 * n) & (ja < 3 * n))
-        def _():
-            k = ja - 2 * n
-            kp = lax.rem(k, KEEP)
-            part[kp] = nn(pick_t[...], slot[k])
-            dest = lax.rem(z + 4, NZ)
-            for i in range(2):
-                value = part[kp, span(dest * BLK + i * HALF, HALF, HALF), :]
-                back_out(i, k, 0, i)[...] = value.astype(BF)
-                back_ring(i, k, 0, i).start()
-
-        jr = t - 5
+                        back_ring(i, k, s - 1).wait_recv()
+                        block = span(dest * BLK, BLK, BLK)
+                        if s == 1:
+                            first = (i * 4 + s) * BLK
+                            for p in range(2):
+                                value = part[k, span(dest * BLK + p * HALF, HALF, HALF), :]
+                                if p == i:
+                                    value = (value.astype(F32) + z_in[i, k, 0, 0:HALF, :].astype(F32)).astype(BF)
+                                ag[AG_SLOTS - n + k, first + p * HALF : first + (p + 1) * HALF, :] = value
+                        else:
+                            value = part[k, block, :].astype(F32) + z_in[i, k, s - 1].astype(F32)
+                            back_out(i, k, s)[...] = value.astype(BF)
+                        back_ring(i, k, s).start()
+
+        jr = t - relay_at
 
         @pl.when((jr >= 0) & (jr < 3 * n))
         def _():
@@ -452,34 +374,32 @@
                 x_arrival(jr, 2 + i).wait_recv()
                 x_copy(jr, 4 + i).start()
 
-        @pl.when((jr >= 0) & (jr < 2 * n))
+        j = t - gather_at
+
+        @pl.when(j == 0)
+        def _():
+            build_picker(z, meta, pick, slot_gate)
+
+        @pl.when((j >= 0) & (j < 2 * n))
         def _():
             for i in range(2):
-                for p in range(2):
-                    for s in range(4 if p == i else 3):
-                        ring(i, jr, s, p, s).wait_send()
-
-        sub_tick(t, 1)
-
-        j = t - 4
-
-        @pl.when(j == 0)
-        def _():
-            build_picker(z, meta, pick, slot_gate)
+                for s in range(4):
+                    ring(i, j, s, s).wait_send()
 
         @pl.when((j >= 4) & (j < 3 * n))
         def _():
             for what in range(4):
                 x_copy(j - 4, what).wait_send()
 
-        @pl.when((j >= 0) & (j < 2 * n))
+        @pl.when(((j >= 0) & (j < back_at)) | ((j >= late_at) & (j < 3 * n)))
         def _():
             plain = (j >= n).astype(F32)
-            rows32[...] = nn(pick[...], ag[lax.rem(j, n)]) * (slot_gate[...] * (1.0 - plain) + plain)
-
-        @pl.when((j >= 2 * n) & (j < 3 * n))
-        def _():
-            block = block_of(j - 2 * n)
+            chunk = j - n * (j // late_at)
+            rows32[...] = nn(pick[...], ag[lax.rem(chunk, AG_SLOTS)]) * (slot_gate[...] * (1.0 - plain) + plain)
+
+        @pl.when((j >= back_at) & (j < late_at))
+        def _():
+            block = block_of(j - back_at)
             rows32[...] = nn(g_gate[...], weights[1, block]) + nn(g_up[...], weights[2, block])
 
         @pl.when((j >= 0) & (j < 3 * n))
@@ -493,18 +413,94 @@
                 for what in {2: (2, 3), 1: (0,), 3: (1,), 0: ()}[d]:
                     x_copy(j, what).start()
 
+        ja = t - ready_at
+
+        @pl.when((ja >= 0) & (ja < 3 * n))
+        def _():
+            for what in (0, 1, 4, 5):
+                x_arrival(ja, what).wait_recv()
+
+        @pl.when((ja >= 1) & (ja < 3 * n + 1))
+        def _():
+            for what in (4, 5):
+                x_copy(ja - 1, what).wait_send()
+
+        for when, step in (
+            (5, lambda: (w_forward(0), w_start(1))),
+            (8, lambda: w_far(0)),
+            (10, lambda: (w_forward(1), w_start(2))),
+            (12, lambda: w_done(0)),
+            (13, lambda: w_far(1)),
+            (14, lambda: w_forward(2)),
+            (16, lambda: (w_done(1), w_far(2))),
+            (18, lambda: w_done(2)),
+        ):
+
+            @pl.when(t == when)
+            def _():
+                step()
+
+        for b in range(2):
+
+            @pl.when(t * 2 + b < steps)
+            def _():
+                activations(t * 2 + b)
+
+        @pl.when(t == gather_at - 1)
+        def _():
+            for b, cols in enumerate(tiles):
+                act_t[0, cols, :] = stage[b, :, 0 : cols.stop - cols.start].T
+
+        @pl.when((j >= 1) & (j < 1 + NZ))
+        def _():
+            block = span((j - 1) * BLK, BLK, BLK)
+            pick_t[block, :] = pick[:, block].T
+
+        @pl.when((ja >= 0) & (ja < n))
+        def _():
+            block = block_of(ja)
+            for b, cols in enumerate(tiles):
+                gh[b, :, 0 : cols.stop - cols.start] += nt(slot[ja], weights[0, block, cols, :])
+
+        @pl.when(ja == n - 1)
+        def _():
+            for b, cols in enumerate(tiles):
+                grad = gh[b, :, 0 : cols.stop - cols.start]
+                g_gate[:, cols] = (grad * g_gate[:, cols].astype(F32)).astype(BF)
+                g_up[:, cols] = (grad * g_up[:, cols].astype(F32)).astype(BF)
+            act_t[1] = g_gate[...].T
+            act_t[2] = g_up[...].T
+
+        @pl.when((ja >= 3) & (ja < n + 3))
+        def _():
+            reduce_block(0, ja - 3, ja - 3)
+
+        @pl.when(((ja >= n) & (ja < back_at)) | ((ja >= late_at) & (ja < 3 * n)))
+        def _():
+            k = ja - n - n * (ja // late_at)
+            reduce_block(1, k, lax.rem(ja, 2 * n))
+            reduce_block(2, k, lax.rem(ja, 2 * n))
+
+        @pl.when((ja >= back_at) & (ja < late_at))
+        def _():
+            k = ja - back_at
+            part[k] = nn(pick_t[...], slot[lax.rem(ja, 2 * n)]).astype(BF)
+            dest = lax.rem(z + 4, NZ)
+            for i in range(2):
+                back_out(i, k, 0)[...] = part[k, span(dest * BLK + i * HALF, HALF, HALF), :]
+                back_ring(i, k, 0).start()
+
         return carry
 
-    lax.fori_loop(0, 3 * n + 10, tick, 0)
+    lax.fori_loop(0, max(sums_at + n + 4 * SUM_LAG, 3 * n + ready_at + 1), tick, 0)
     for i in range(2):
         for s in range(4):
             ring_meta(i, s, s).wait_send()
 
     def ended(k, carry):
         for i in range(2):
-            for p in range(2):
-                for s in range(0 if p == i else 1, 4):
-                    back_ring(i, k, s, p).wait_send()
+            for s in range(4):
+                back_ring(i, k, s).wait_send()
         return carry
 
     lax.fori_loop(0, n, ended, 0)
@@ -519,14 +515,10 @@
         y_copy(m, 3).wait_send()
 
 
-def hand_out(rows, grads, out, grad_gate, grad_up, grad_down, sem):
-    copies = [pltpu.make_async_copy(rows, out, sem.at[0])]
+def hand_out(rows, grads, out, grad_gate, grad_up, grad_down):
+    out[...] = rows[...]
     for m, to in ((1, grad_gate), (2, grad_up), (0, grad_down)):
-        copies.append(pltpu.make_async_copy(grads.at[m], to, sem.at[1 + m]))
-    for copy in copies:
-        copy.start()
-    for copy in copies:
-        copy.wait()
+        to[...] = grads[m]
 
 
 def shards(tokens, cotangent, expert_ids, gate_values, saved_pre, w_gate, w_up, w_down):
@@ -545,17 +537,17 @@
         out_specs=(vmem, vmem),
         scratch_shapes=[
             pltpu.VMEM((NZ, 16, BLK), F32),
-            pltpu.VMEM((n, NZ * BLK, CH), BF),
+            pltpu.VMEM((AG_SLOTS, NZ * BLK, CH), BF),
             pltpu.VMEM((2 * n, SLOTS, CH), BF),
             pltpu.VMEM((4, SLOTS, CH), BF),
             pltpu.VMEM((n, GRP, CH), BF),
             pltpu.VMEM((SLOTS, NZ * BLK), BF),
             pltpu.VMEM((NZ * BLK, SLOTS), BF),
             pltpu.VMEM((SLOTS, 1), F32),
-            pltpu.VMEM((KEEP, NZ * BLK, CH), F32),
+            pltpu.VMEM((n, NZ * BLK, CH), BF),
             pltpu.VMEM((2, n, 4, BLK, CH), BF),
             pltpu.VMEM((3, n, hidden, CH), BF),
-            pltpu.VMEM((SLOTS, hidden), BF),
+            pltpu.VMEM((3, SLOTS, CH), F32),
             pltpu.VMEM((SLOTS, hidden), BF),
             pltpu.VMEM((SLOTS, hidden), BF),
             pltpu.VMEM((3, hidden, SLOTS), BF),
@@ -568,14 +560,14 @@
             pltpu.VMEM((3, 2, hidden, CH), BF),
             pltpu.VMEM((3, hidden, CH), BF),
             pltpu.VMEM((3, 2, hidden, CH), BF),
-            dma((2, n, 4, 2)),
-            dma((2, n, 4, 2)),
+            dma((2, 2 * n, 4)),
+            dma((2, 2 * n, 4)),
             dma((2, 4)),
             dma((2, 4)),
             dma((n, 6)),
             dma((n, 6)),
-            dma((2, n, 4, 2)),
-            dma((2, n, 4, 2)),
+            dma((2, n, 4)),
+            dma((2, n, 4)),
             dma((3, 8)),
             dma((3, 8)),
             dma((3, NY)),
@@ -593,9 +585,8 @@
     out, grad_gate, grad_up, grad_down = pl.pallas_call(
         hand_out,
         out_shape=(shape((BLK, width), BF), *[shape((hidden, CH), BF)] * 3),
-        in_specs=[hbm] * 2,
-        out_specs=(hbm,) * 4,
-        scratch_shapes=[dma((4,))],
+        in_specs=[vmem] * 2,
+        out_specs=(vmem,) * 4,
         name="hand_out",
     )(rows, grads)
     return (out, grad_gate.T[None], grad_up.T[None], grad_down[None])

time: 240 us -> 183 us (0.76)
  Pallas kernels: 240 us -> 181 us
    pallas_call x1, Pallas kernels: 49.8 us -> 2.57 us  [shards(): pl.pallas_call(hand_out, out_shape=(shape((BLK, width), BF), *[shape((hid...]
    pallas_call x1, Pallas kernels: 190 us -> 179 us  [shards(): pl.pallas_call(kernel, out_shape=(shape((BLK, width), BF), shape((3, hidd...]
where the time goes in v4:
time: 183 us; the launch traced here: 182 us
  Pallas kernels  181 us (99%)
    pallas_call x1, Pallas kernels, shards(): pl.pallas_call(kernel, out_shape=(shape((BLK, width), BF), shape((3, hidd...  179 us

profile of v4, /device:TPU:2, one launch (start us, length us, event | category | flops | bytes accessed | tf_op | source)
XLA Modules:
  0.0 182.0 jit_solution(14387718800212435209)
XLA Ops:
  0.6 178.7 %expert_backward.1 = (bf16[128,2048]{1,0:T(8,128)(2,1)}, bf16[3,704,256]{2,1,0:T(8,128)(2,1)}) custom-call(bf16[128,2048]{1,0:T(8,128)(2,1)} %cot.1, bf16[128,2048]{1,0:T(8,128)(2,1)} %tok.1, s32[6,128]{1,0:T(8,128)} %bitcast.28, f32[6,128]{1,0:T(8,128)} %bitcast.29, bf16[832,1408]{1,0:T(8,128)(2,1)} %bitcast.21, bf16[704,256]{1,0:T(8,128)(2,1)} %bitcast.22, ...), custom_call_target="tpu_custom_call" | custom-call | flops 25999998976 | bytes 10485760 | tf_op jit(solution)/shard_map/expert_backward/pallas_call | solution.py:533
  179.4 2.6 %hand_out.1 = (bf16[128,2048]{1,0:T(8,128)(2,1)}, bf16[704,256]{1,0:T(8,128)(2,1)}, bf16[704,256]{1,0:T(8,128)(2,1)}, bf16[704,256]{1,0:T(8,128)(2,1)}) custom-call(bf16[128,2048]{1,0:T(8,128)(2,1)} %get-tuple-element.10.rows, bf16[3,704,256]{2,1,0:T(8,128)(2,1)} %get-tuple-element.11.grads), custom_call_target="tpu_custom_call" | custom-call | tf_op jit(solution)/shard_map/hand_out/pallas_call | solution.py:585

commit v5 on v4

--- a/solution.py
+++ b/solution.py
@@ -15,7 +15,7 @@
 CH = 256
 VIA = 112
 LAG = 2
-X_LAG = 2
+X_LAG = 1
 SUM_LAG = 2
 AG_SLOTS = 12
 HALF = BLK // 2
@@ -300,9 +300,10 @@
         gh[b] = jnp.zeros((SLOTS, CH), F32)
 
     gather_at = 4 * LAG
+    per_tick = -(-steps // gather_at)
     relay_at = gather_at + X_LAG
     ready_at = gather_at + 2 * X_LAG
-    early = n // 2
+    early = n // 4
     back_at = n + early
     late_at = back_at + n
     sums_at = back_at + ready_at
@@ -426,25 +427,24 @@
                 x_copy(ja - 1, what).wait_send()
 
         for when, step in (
-            (5, lambda: (w_forward(0), w_start(1))),
-            (8, lambda: w_far(0)),
-            (10, lambda: (w_forward(1), w_start(2))),
-            (12, lambda: w_done(0)),
-            (13, lambda: w_far(1)),
-            (14, lambda: w_forward(2)),
-            (16, lambda: (w_done(1), w_far(2))),
-            (18, lambda: w_done(2)),
+            (3, lambda: (w_forward(0), w_start(1))),
+            (5, lambda: w_far(0)),
+            (6, lambda: (w_forward(1), w_start(2))),
+            (ready_at, lambda: (w_done(0), w_far(1))),
+            (ready_at + 1, lambda: w_forward(2)),
+            (ready_at + 3, lambda: (w_done(1), w_far(2))),
+            (ready_at + 5, lambda: w_done(2)),
         ):
 
             @pl.when(t == when)
             def _():
                 step()
 
-        for b in range(2):
-
-            @pl.when(t * 2 + b < steps)
+        for b in range(per_tick):
+
+            @pl.when((t < gather_at) & (t * per_tick + b < steps))
             def _():
-                activations(t * 2 + b)
+                activations(t * per_tick + b)
 
         @pl.when(t == gather_at - 1)
         def _():

time: 183 us -> 180 us (0.984)
  Pallas kernels: 181 us -> 179 us
    pallas_call x1, Pallas kernels: 179 us -> 177 us  [shards(): pl.pallas_call(kernel, out_shape=(shape((BLK, width), BF), shape((3, hidd...]
where the time goes in v5:
time: 180 us
  Pallas kernels  179 us (99%)
    pallas_call x1, Pallas kernels, shards(): pl.pallas_call(kernel, out_shape=(shape((BLK, width), BF), shape((3, hidd...  177 us

profile of v5, /device:TPU:2, one launch (start us, length us, event | category | flops | bytes accessed | tf_op | source)
XLA Modules:
  0.0 179.8 jit_solution(2251233572366210665)
XLA Ops:
  0.6 176.6 %expert_backward.1 = (bf16[128,2048]{1,0:T(8,128)(2,1)}, bf16[3,704,256]{2,1,0:T(8,128)(2,1)}) custom-call(bf16[128,2048]{1,0:T(8,128)(2,1)} %cot.1, bf16[128,2048]{1,0:T(8,128)(2,1)} %tok.1, s32[6,128]{1,0:T(8,128)} %bitcast.28, f32[6,128]{1,0:T(8,128)} %bitcast.29, bf16[832,1408]{1,0:T(8,128)(2,1)} %bitcast.21, bf16[704,256]{1,0:T(8,128)(2,1)} %bitcast.22, ...), custom_call_target="tpu_custom_call" | custom-call | flops 25999998976 | bytes 10485760 | tf_op jit(solution)/shard_map/expert_backward/pallas_call | solution.py:533
  177.2 2.6 %hand_out.1 = (bf16[128,2048]{1,0:T(8,128)(2,1)}, bf16[704,256]{1,0:T(8,128)(2,1)}, bf16[704,256]{1,0:T(8,128)(2,1)}, bf16[704,256]{1,0:T(8,128)(2,1)}) custom-call(bf16[128,2048]{1,0:T(8,128)(2,1)} %get-tuple-element.10.rows, bf16[3,704,256]{2,1,0:T(8,128)(2,1)} %get-tuple-element.11.grads), custom_call_target="tpu_custom_call" | custom-call | tf_op jit(solution)/shard_map/hand_out/pallas_call | solution.py:585

commit v6 on v5

--- a/solution.py
+++ b/solution.py
@@ -309,6 +309,14 @@
     sums_at = back_at + ready_at
 
     def tick(t, carry):
+        jr = t - relay_at
+
+        @pl.when((jr >= 0) & (jr < 3 * n))
+        def _():
+            for i in range(2):
+                x_arrival(jr, 2 + i).wait_recv()
+                x_copy(jr, 4 + i).start()
+
         for s in (4, 3, 2, 1, 0):
             j = t - LAG * s
 
@@ -366,14 +374,6 @@
                             value = part[k, block, :].astype(F32) + z_in[i, k, s - 1].astype(F32)
                             back_out(i, k, s)[...] = value.astype(BF)
                         back_ring(i, k, s).start()
-
-        jr = t - relay_at
-
-        @pl.when((jr >= 0) & (jr < 3 * n))
-        def _():
-            for i in range(2):
-                x_arrival(jr, 2 + i).wait_recv()
-                x_copy(jr, 4 + i).start()
 
         j = t - gather_at
 

time: 180 us -> 181 us (level)
  no operation moved by 1% of the time
where the time goes in v6:
time: 181 us; the launch traced here: 180 us
  Pallas kernels  180 us (99%)
    pallas_call x1, Pallas kernels, shards(): pl.pallas_call(kernel, out_shape=(shape((BLK, width), BF), shape((3, hidd...  177 us

profile of v6, /device:TPU:2, one launch (start us, length us, event | category | flops | bytes accessed | tf_op | source)
XLA Modules:
  0.0 180.3 jit_solution(8207477485750172189)
XLA Ops:
  0.6 177.1 %expert_backward.1 = (bf16[128,2048]{1,0:T(8,128)(2,1)}, bf16[3,704,256]{2,1,0:T(8,128)(2,1)}) custom-call(bf16[128,2048]{1,0:T(8,128)(2,1)} %cot.1, bf16[128,2048]{1,0:T(8,128)(2,1)} %tok.1, s32[6,128]{1,0:T(8,128)} %bitcast.28, f32[6,128]{1,0:T(8,128)} %bitcast.29, bf16[832,1408]{1,0:T(8,128)(2,1)} %bitcast.21, bf16[704,256]{1,0:T(8,128)(2,1)} %bitcast.22, ...), custom_call_target="tpu_custom_call" | custom-call | flops 25999998976 | bytes 10485760 | tf_op jit(solution)/shard_map/expert_backward/pallas_call | solution.py:533
  177.7 2.6 %hand_out.1 = (bf16[128,2048]{1,0:T(8,128)(2,1)}, bf16[704,256]{1,0:T(8,128)(2,1)}, bf16[704,256]{1,0:T(8,128)(2,1)}, bf16[704,256]{1,0:T(8,128)(2,1)}) custom-call(bf16[128,2048]{1,0:T(8,128)(2,1)} %get-tuple-element.10.rows, bf16[3,704,256]{2,1,0:T(8,128)(2,1)} %get-tuple-element.11.grads), custom_call_target="tpu_custom_call" | custom-call | tf_op jit(solution)/shard_map/hand_out/pallas_call | solution.py:585
